TPU v7x, 256 devices: a whole 4x4x8 slice. The times are simulated.
256 devices in a mesh: row: 16 (over x, z_hi), col: 16 (over z_lo, y, core).
Axes of the slice: x: 4, y: 4, z: 8 (z_hi: 4, z_lo: 2; z = z_hi * 2 + z_lo), core: 2. Of those that a mesh axis runs over, the one named last changes fastest.
Arguments:
- row_locs: float32 [2, 32768], P(None, 'row'), may hold values from 0 to 1
- panel_locs: float32 [2, 512], replicated, may hold values from 0 to 1
- prior_panel: float32 [32768, 512], P('row', 'col'), may hold values from -0.625 to 0.625
- prior_trail: float32 [32768, 8192], P('row', 'col'), may hold values from -1.25 to 1.25
Outputs:
- panel_factor: float32 [32768, 512], P('row')
- trailing: float32 [32768, 8192], P('row', 'col')
All inputs are finite; a program needn't handle non-finite values.
Results may differ from a plain program's by a relative error of at most 0.0003.
Values sent between devices are 32-bit elements; how exact they have to be, the bound alone decides.
A program may use at most 64 MiB of HBM per device.

v0:
```python
import jax
import jax.numpy as jnp
from jax import lax
from jax.experimental import pallas as pl
from jax.experimental.pallas import tpu as pltpu
from jax.sharding import PartitionSpec as P

STRIP = 16
BLOCK = 128
f32, bf16 = jnp.float32, jnp.bfloat16


def exp_distance(dx, dy):
    d2 = dx * dx + dy * dy
    return jnp.exp(d2 * lax.rsqrt(jnp.maximum(d2, 1e-30)) * -10.0)


def split3(x):
    a = x.astype(bf16)
    r = x - a.astype(f32)
    b = r.astype(bf16)
    return a, b, (r - b.astype(f32)).astype(bf16)


def lanes_of(x, j):
    return jnp.broadcast_to(x[:, j : j + 1], (8, BLOCK))


def row_of(x, i):
    return jnp.broadcast_to(x[i : i + 1, :], (8, BLOCK))


def invert_block(d_ref):
    lane = lax.broadcasted_iota(jnp.int32, (8, BLOCK), 1)
    sub = lax.broadcasted_iota(jnp.int32, (8, BLOCK), 0)
    groups = STRIP // 8
    for strip in range(BLOCK // STRIP):
        base = strip * STRIP
        rows = [d_ref[base + 8 * g : base + 8 * g + 8, :] for g in range(groups)]
        cols = [[lanes_of(rows[g], base + j) for g in range(groups)] for j in range(STRIP)]
        scale = [jnp.zeros((8, BLOCK), f32)] * groups
        for i in range(STRIP):
            h, q = i // 8, i % 8
            pivot = row_of(cols[i][h], q)
            inv_pivot = 1.0 / pivot
            scale[h] = jnp.where(sub == q, lax.rsqrt(pivot), scale[h])
            f = [None] * groups
            f[h] = jnp.where(sub > q, cols[i][h], 0.0) * inv_pivot
            for g in range(h + 1, groups):
                f[g] = cols[i][g] * inv_pivot
            for j in range(i + 1, STRIP):
                t = row_of(cols[j][h], q)
                for g in range(h, groups):
                    cols[j][g] = cols[j][g] - f[g] * t
            rows[h] = jnp.where(lane == base + i, jnp.where(sub == q, 1.0, 0.0), rows[h])
            for g in range(h + 1, groups):
                rows[g] = jnp.where(lane == base + i, 0.0, rows[g])
            t = row_of(rows[h], q)
            for g in range(h, groups):
                rows[g] = rows[g] - f[g] * t
        for g in range(groups):
            above = (lane > base + 8 * g + sub) & (lane < base + STRIP)
            rows[g] = jnp.where(above, 0.0, rows[g]) * scale[g]
            d_ref[base + 8 * g : base + 8 * g + 8, :] = rows[g]
        first = base + STRIP
        if first < BLOCK:
            a, b, c = split3(jnp.concatenate(rows, axis=0))
            left = jnp.concatenate([a, a, b, a, b, c], axis=0)
            right = jnp.concatenate([a, b, a, c, b, a], axis=0)
            update = lax.dot_general(left, right, (((0,), (0,)), ((), ())), preferred_element_type=f32)
            wide = lax.broadcasted_iota(jnp.int32, (BLOCK - first, BLOCK), 1)
            old = jnp.where((wide >= base) & (wide < first), 0.0, d_ref[first:, :])
            d_ref[first:, :] = old - update[first:, :]


def hdot(a, b, dims):
    return lax.dot_general(a, b, (dims, ((), ())), precision=lax.Precision.HIGHEST, preferred_element_type=f32)


def fill_matrix(locs_ref, m_ref, n):
    blocks = n // BLOCK
    eye = lax.broadcasted_iota(jnp.int32, (BLOCK, BLOCK), 0) == lax.broadcasted_iota(jnp.int32, (BLOCK, BLOCK), 1)
    for bi in range(blocks):
        col = [jnp.transpose(jnp.broadcast_to(locs_ref[c : c + 1, bi * BLOCK : (bi + 1) * BLOCK], (BLOCK, BLOCK))) for c in (0, 1)]
        for bj in range(blocks):
            at = (slice(bi * BLOCK, (bi + 1) * BLOCK), slice(bj * BLOCK, (bj + 1) * BLOCK))
            if bj < bi:
                m_ref[at] = jnp.zeros((BLOCK, BLOCK), f32)
                continue
            row = [locs_ref[c : c + 1, bj * BLOCK : (bj + 1) * BLOCK] for c in (0, 1)]
            value = exp_distance(col[0] - row[0], col[1] - row[1])
            if bi == bj:
                value = value + jnp.where(eye, 0.1, 0.0)
            m_ref[at] = value


def chol_kernel(locs_ref, inv_ref, m_ref, d_ref):
    n = locs_ref.shape[1]
    blocks = n // BLOCK
    fill_matrix(locs_ref, m_ref, n)
    lower = lax.broadcasted_iota(jnp.int32, (BLOCK, BLOCK), 0) >= lax.broadcasted_iota(jnp.int32, (BLOCK, BLOCK), 1)
    lane_block = lax.broadcasted_iota(jnp.int32, (BLOCK, n), 1) // BLOCK

    def one_block(k, carry):
        mine = pl.ds(pl.multiple_of(k * BLOCK, BLOCK), BLOCK)
        d_ref[...] = m_ref[mine, mine]
        invert_block(d_ref)
        w = jnp.where(lower, d_ref[...], 0.0)
        row = hdot(w, m_ref[mine, :], ((1,), (0,)))
        m_ref[mine, :] = row
        m_ref[mine, mine] = w
        row = m_ref[mine, :]
        inv_ref[mine, :] = jnp.where(lane_block <= k, row, 0.0)

        def below(i, carry):
            his = pl.ds(pl.multiple_of(i * BLOCK, BLOCK), BLOCK)
            update = hdot(m_ref[mine, his], row, ((0,), (0,)))
            m_ref[his, :] = jnp.where(lane_block == k, 0.0, m_ref[his, :]) - update
            return carry

        return lax.fori_loop(k + 1, blocks, below, carry)

    lax.fori_loop(0, blocks, one_block, 0)


def invert_factor(locs):
    n = locs.shape[1]
    return pl.pallas_call(
        chol_kernel,
        out_shape=jax.ShapeDtypeStruct((n, n), f32),
        in_specs=[pl.BlockSpec(memory_space=pltpu.VMEM)],
        out_specs=pl.BlockSpec(memory_space=pltpu.VMEM),
        scratch_shapes=[pltpu.VMEM((n, n), f32), pltpu.VMEM((BLOCK, BLOCK), f32)],
        compiler_params=pltpu.CompilerParams(vmem_limit_bytes=32 * 2**20),
        cost_estimate=pl.CostEstimate(flops=2 * n**3, bytes_accessed=8 * n * n, transcendentals=n * n),
        name="invert_factor",
    )(locs)


ROW_TILE = 256


def split2(x):
    high = x.astype(bf16)
    return high, (x - high.astype(f32)).astype(bf16)


def dot3(left, right):
    def one(a, b):
        return lax.dot_general(a, b, (((1,), (1,)), ((), ())), preferred_element_type=f32)

    return one(left[0], right[0]) + (one(left[0], right[1]) + one(left[1], right[0]))


def across(row):
    return jnp.transpose(jnp.broadcast_to(row, (BLOCK, BLOCK)))


def trailing_kernel(panel_ref, tile_ref, inv_ref, row_locs_ref, col_locs_ref, prior_ref, factor_ref, out_ref, inv_h, inv_l, col_h, col_l):
    step = pl.program_id(0)
    width = out_ref.shape[1]

    @pl.when(step == 0)
    def _():
        high, low = split2(inv_ref[...])
        inv_h[...] = high
        inv_l[...] = low
        col_factor = dot3(split2(jnp.transpose(tile_ref[...])), (high, low))
        col_h[...], col_l[...] = split2(col_factor)

    factor = dot3(split2(jnp.transpose(panel_ref[...])), (inv_h[...], inv_l[...]))
    factor_ref[...] = factor
    update = dot3(split2(factor), (col_h[...], col_l[...]))
    on_diagonal = lax.axis_index("row") == lax.axis_index("col")
    for part in range(ROW_TILE // BLOCK):
        rows = slice(part * BLOCK, (part + 1) * BLOCK)
        xr = across(row_locs_ref[0:1, rows])
        yr = across(row_locs_ref[1:2, rows])
        for block in range(width // BLOCK):
            cols = slice(block * BLOCK, (block + 1) * BLOCK)
            value = exp_distance(xr - col_locs_ref[0:1, cols], yr - col_locs_ref[1:2, cols])
            i = lax.broadcasted_iota(jnp.int32, (BLOCK, BLOCK), 0) + (step * ROW_TILE + part * BLOCK)
            j = lax.broadcasted_iota(jnp.int32, (BLOCK, BLOCK), 1) + block * BLOCK
            value = value + jnp.where((i == j) & on_diagonal, 0.1, 0.0)
            out_ref[rows, cols] = value - prior_ref[rows, cols] - update[rows, cols]


def trailing_update(panel_t, tile_t, inv_lower, row_locs, col_locs, prior_trail):
    depth, rows = panel_t.shape
    width = prior_trail.shape[1]
    whole = lambda shape: pl.BlockSpec(shape, lambda i: (0, 0))
    return pl.pallas_call(
        trailing_kernel,
        grid=(rows // ROW_TILE,),
        out_shape=(jax.ShapeDtypeStruct((rows, depth), f32), jax.ShapeDtypeStruct((rows, width), f32)),
        in_specs=[
            pl.BlockSpec((depth, ROW_TILE), lambda i: (0, i)),
            whole((depth, width)),
            whole((depth, depth)),
            pl.BlockSpec((2, ROW_TILE), lambda i: (0, i)),
            whole((2, width)),
            pl.BlockSpec((ROW_TILE, width), lambda i: (i, 0)),
        ],
        out_specs=(pl.BlockSpec((ROW_TILE, depth), lambda i: (i, 0)), pl.BlockSpec((ROW_TILE, width), lambda i: (i, 0))),
        scratch_shapes=[pltpu.VMEM((depth, depth), bf16)] * 2 + [pltpu.VMEM((width, depth), bf16)] * 2,
        compiler_params=pltpu.CompilerParams(vmem_limit_bytes=60 * 2**20),
        cost_estimate=pl.CostEstimate(flops=12 * rows * depth * width, bytes_accessed=16 * rows * width, transcendentals=2 * rows * width),
        name="trailing_update",
    )(panel_t, tile_t, inv_lower, row_locs, col_locs, prior_trail)


def covariance(left_locs, right_locs):
    return exp_distance(left_locs[0][:, None] - right_locs[0][None, :], left_locs[1][:, None] - right_locs[1][None, :])


def body(row_locs, panel_locs, prior_panel, prior_trail):
    tile = panel_locs.shape[1]
    width = prior_panel.shape[1]
    n = lax.axis_size("col")
    my_panel_locs = lax.dynamic_slice_in_dim(panel_locs, lax.axis_index("col") * width, width, 1)
    part = covariance(my_panel_locs, row_locs) - prior_panel.T
    swap = [(r * n + c, c * n + r) for r in range(n) for c in range(n)]
    packed = jnp.concatenate([part[:, :tile], row_locs[:, :tile], jnp.zeros((6, tile), f32)], axis=0)
    packed = lax.ppermute(packed, ("row", "col"), swap)
    tile_t = lax.all_gather(packed[:width], "row", axis=0, tiled=True)
    panel_t = lax.all_gather(part, "col", axis=0, tiled=True)
    inv_lower = invert_factor(panel_locs)
    return trailing_update(panel_t, tile_t, inv_lower, row_locs, packed[width : width + 2], prior_trail)


def solution(mesh):
    in_specs = (P(None, "row"), P(), P("row", "col"), P("row", "col"))
    out_specs = (P("row", None), P("row", "col"))
    return jax.shard_map(body, mesh=mesh, in_specs=in_specs, out_specs=out_specs, check_vma=False)
```

profile of v0, /device:TPU:1, one launch (start us, length us, event | category | flops | bytes accessed | tf_op | source)
XLA Modules:
  0.0 145.1 jit_solution(13944593518992386577)
XLA Ops:
  7.2 0.0 all-gather.5.cloned.1.call-start
  7.2 0.7 slice.29
  7.9 0.8 fusion
  8.7 0.8 constant_dynamic-slice_fusion
  9.5 1.1 bitcast_subtract_fusion
  10.6 0.0 copy-start.2
  10.7 0.1 pad.2.clone
  10.7 0.1 maximum_maximum_fusion
  10.8 6.3 %collective-permute-start = (f32[40,512]{1,0:T(8,128)S(1)}, f32[40,512]{1,0:T(8,128)S(1)}, u32[]{:S(2)}, u32[]{:S(2)}) collective-permute-start(f32[40,512]{1,0:T(8,128)S(1)} %maximum_maximum_fusion), channel_id=1, source_target_pairs={{0,0},{1,16},{2,32},{3,48},{4,64},{5,80},{6,96},{7,112},{8,128},{9... | collective-permute-start | bytes 245768 | tf_op jit(solution)/shard_map/ppermute | solution.py:224
  17.1 2.1 %collective-permute-done = f32[40,512]{1,0:T(8,128)S(1)} collective-permute-done((f32[40,512]{1,0:T(8,128)S(1)}, f32[40,512]{1,0:T(8,128)S(1)}, u32[]{:S(2)}, u32[]{:S(2)}) %collective-permute-start) | collective-permute-done | bytes 81952 | tf_op jit(solution)/shard_map/ppermute | solution.py:224
  19.2 0.6 slice.33
  19.8 0.0 all-gather.5.cloned.1.call-update
  19.9 0.0 all-gather.3.cloned.1.call-start
  19.9 0.0 copy-done.2
  19.9 0.7 all-gather.3.cloned.1.call-update
  20.6 0.0 copy-start.1
  20.6 0.7 copy-done.1
  21.3 18.2 %invert_factor.1.inv_ref = f32[512,512]{1,0:T(8,128)S(1)} custom-call(f32[2,512]{1,0:T(2,128)S(1)} %copy-done.1), custom_call_target="tpu_custom_call" | custom-call | flops 268435456 | bytes 2097152 | tf_op jit(solution)/shard_map/invert_factor/pallas_call | solution.py:128
  39.5 0.0 copy-start
  39.5 1.0 copy-done
  40.5 0.6 slice.34.col_locs_ref
  41.1 41.4 %all-gather.5.cloned.1.call-done.tile_ref = f32[512,512]{1,0:T(8,128)} async-done(((f32[32,512]{1,0:T(8,128)}), f32[512,512]{1,0:T(8,128)}) %all-gather.5.cloned.1.call-update) | async-done | bytes 1048592 | tf_op jit(solution)/shard_map/all_gather | solution.py:225
  82.5 41.3 %all-gather.3.cloned.1.call-done.panel_ref = f32[512,2048]{1,0:T(8,128)} async-done(((f32[32,2048]{1,0:T(8,128)}), f32[512,2048]{1,0:T(8,128)}) %all-gather.3.cloned.1.call-update) | async-done | bytes 4194320 | tf_op jit(solution)/shard_map/all_gather | solution.py:226
  123.8 14.4 %trailing_update.1 = (f32[2048,512]{1,0:T(8,128)}, f32[2048,512]{1,0:T(8,128)}) custom-call(f32[512,2048]{1,0:T(8,128)} %all-gather.3.cloned.1.call-done.panel_ref, f32[512,512]{1,0:T(8,128)} %all-gather.5.cloned.1.call-done.tile_ref, f32[512,512]{1,0:T(8,128)} %copy-done, f32[2,2048]{1,0:T(2,128)} %row_locs_ref.1, f32[2,512]{1,0:T(2,128)} %slice.34.col_locs_ref, ...), custom_call_target="tpu_custom_call" | custom-call | flops 6442450944 | bytes 16777216 | tf_op jit(solution)/shard_map/trailing_update/pallas_call | solution.py:192
  (3 shorter events, 0.0 us)
Async XLA Ops:
  7.2 75.4 %all-gather.5.cloned.1.call-start = ((), (), s32[]{:S(2)}) async-start(), calls=%async_computation.1 | async-start | bytes 1114112 | tf_op jit(solution)/shard_map/all_gather | solution.py:225
  10.6 9.3 %copy-start.2 = (f32[32,2048]{1,0:T(8,128)}, f32[32,2048]{1,0:T(8,128)S(1)}, u32[]{:S(2)}) copy-start(f32[32,2048]{1,0:T(8,128)S(1)} %bitcast_subtract_fusion) | copy-start | bytes 786436
  10.8 8.4 %collective-permute-start = (f32[40,512]{1,0:T(8,128)S(1)}, f32[40,512]{1,0:T(8,128)S(1)}, u32[]{:S(2)}, u32[]{:S(2)}) collective-permute-start(f32[40,512]{1,0:T(8,128)S(1)} %maximum_maximum_fusion), channel_id=1, source_target_pairs={{0,0},{1,16},{2,32},{3,48},{4,64},{5,80},{6,96},{7,112},{8,128},{9... | collective-permute-start | bytes 245768 | tf_op jit(solution)/shard_map/ppermute | solution.py:224
  19.9 104.0 %all-gather.3.cloned.1.call-start = ((), (), s32[]{:S(2)}) async-start(), calls=%async_computation | async-start | bytes 4456448 | tf_op jit(solution)/shard_map/all_gather | solution.py:226
  20.6 0.7 copy-start.1
  39.5 1.0 copy-start
Sparse Core Ops, SparseCore 0:
  20.0 62.4 all-gather.4
  84.9 38.8 all-gather.2
where the time goes:
time: 146 us; the launch traced here: 145 us
  waiting for transfers between devices  85.5 us (59%)
  Pallas kernels  32.6 us (22%)
  between operations  14.1 us (10%)
  starting transfers between devices  6.36 us (4%)
  local copies, waits for them, and re-layouts  5.25 us (4%)
    all_gather x1, waiting for transfers between devices, body(): tile_t = lax.all_gather(packed[:width], 'row', axis=0, tiled=True)  41.4 us
    all_gather x1, waiting for transfers between devices, body(): panel_t = lax.all_gather(part, 'col', axis=0, tiled=True)  41.3 us
    pallas_call x1, Pallas kernels, invert_factor(): pl.pallas_call(chol_kernel, out_shape=jax.ShapeDtypeStruct((n, n), f32),...  18.2 us
    pallas_call x1, Pallas kernels, trailing_update(): pl.pallas_call(trailing_kernel, grid=(rows // ROW_TILE,), out_shape=(jax....  14.4 us
    ppermute x1, starting transfers between devices, body(): packed = lax.ppermute(packed, ('row', 'col'), swap)  6.28 us
  transfers between devices with their start and end apart: 3, of which 3 were waited for; matrix products, arithmetic and copies ran while one was open for 0% of the time, Pallas kernels for 13%

commit v1 on v0

--- a/solution.py
+++ b/solution.py
@@ -7,6 +7,7 @@
 
 STRIP = 16
 BLOCK = 128
+VMEM_A = 60 * 2**20
 f32, bf16 = jnp.float32, jnp.bfloat16
 
 
@@ -94,49 +95,6 @@
             m_ref[at] = value
 
 
-def chol_kernel(locs_ref, inv_ref, m_ref, d_ref):
-    n = locs_ref.shape[1]
-    blocks = n // BLOCK
-    fill_matrix(locs_ref, m_ref, n)
-    lower = lax.broadcasted_iota(jnp.int32, (BLOCK, BLOCK), 0) >= lax.broadcasted_iota(jnp.int32, (BLOCK, BLOCK), 1)
-    lane_block = lax.broadcasted_iota(jnp.int32, (BLOCK, n), 1) // BLOCK
-
-    def one_block(k, carry):
-        mine = pl.ds(pl.multiple_of(k * BLOCK, BLOCK), BLOCK)
-        d_ref[...] = m_ref[mine, mine]
-        invert_block(d_ref)
-        w = jnp.where(lower, d_ref[...], 0.0)
-        row = hdot(w, m_ref[mine, :], ((1,), (0,)))
-        m_ref[mine, :] = row
-        m_ref[mine, mine] = w
-        row = m_ref[mine, :]
-        inv_ref[mine, :] = jnp.where(lane_block <= k, row, 0.0)
-
-        def below(i, carry):
-            his = pl.ds(pl.multiple_of(i * BLOCK, BLOCK), BLOCK)
-            update = hdot(m_ref[mine, his], row, ((0,), (0,)))
-            m_ref[his, :] = jnp.where(lane_block == k, 0.0, m_ref[his, :]) - update
-            return carry
-
-        return lax.fori_loop(k + 1, blocks, below, carry)
-
-    lax.fori_loop(0, blocks, one_block, 0)
-
-
-def invert_factor(locs):
-    n = locs.shape[1]
-    return pl.pallas_call(
-        chol_kernel,
-        out_shape=jax.ShapeDtypeStruct((n, n), f32),
-        in_specs=[pl.BlockSpec(memory_space=pltpu.VMEM)],
-        out_specs=pl.BlockSpec(memory_space=pltpu.VMEM),
-        scratch_shapes=[pltpu.VMEM((n, n), f32), pltpu.VMEM((BLOCK, BLOCK), f32)],
-        compiler_params=pltpu.CompilerParams(vmem_limit_bytes=32 * 2**20),
-        cost_estimate=pl.CostEstimate(flops=2 * n**3, bytes_accessed=8 * n * n, transcendentals=n * n),
-        name="invert_factor",
-    )(locs)
-
-
 ROW_TILE = 256
 
 
@@ -209,23 +167,208 @@
     )(panel_t, tile_t, inv_lower, row_locs, col_locs, prior_trail)
 
 
-def covariance(left_locs, right_locs):
-    return exp_distance(left_locs[0][:, None] - right_locs[0][None, :], left_locs[1][:, None] - right_locs[1][None, :])
+MESH = pl.DeviceIdType.MESH
+
+
+def invert_step(k, blocks, m_ref, d_ref, inv_ref):
+    n = m_ref.shape[1]
+    lower = lax.broadcasted_iota(jnp.int32, (BLOCK, BLOCK), 0) >= lax.broadcasted_iota(jnp.int32, (BLOCK, BLOCK), 1)
+    lane_block = lax.broadcasted_iota(jnp.int32, (BLOCK, n), 1) // BLOCK
+    mine = pl.ds(pl.multiple_of(k * BLOCK, BLOCK), BLOCK)
+    d_ref[...] = m_ref[mine, mine]
+    invert_block(d_ref)
+    w = jnp.where(lower, d_ref[...], 0.0)
+    m_ref[mine, :] = hdot(w, m_ref[mine, :], ((1,), (0,)))
+    m_ref[mine, mine] = w
+    row = m_ref[mine, :]
+    inv_ref[mine, :] = jnp.where(lane_block <= k, row, 0.0)
+
+    def below(i, carry):
+        his = pl.ds(pl.multiple_of(i * BLOCK, BLOCK), BLOCK)
+        update = hdot(m_ref[mine, his], row, ((0,), (0,)))
+        m_ref[his, :] = jnp.where(lane_block == k, 0.0, m_ref[his, :]) - update
+        return carry
+
+    lax.fori_loop(k + 1, blocks, below, 0)
+
+
+def gather_kernel(
+    locs_ref, row_locs_ref, prior_ref,
+    panel_ref, tile_ref, inv_ref, col_locs_ref,
+    m_ref, d_ref, part_ref, turn_ref,
+    panel_send, panel_recv, tile_send, tile_recv, swap_send, locs_recv, own_sem,
+):
+    n = locs_ref.shape[1]
+    width, rows = prior_ref.shape
+    tile = col_locs_ref.shape[1]
+    blocks = n // BLOCK
+    row, col = lax.axis_index("row"), lax.axis_index("col")
+    x, z_hi = lax.div(row, 4), lax.rem(row, 4)
+    z_lo, y, core = lax.div(col, 8), lax.rem(lax.div(col, 2), 4), lax.rem(col, 2)
+
+    def col_of(a, b, c):
+        return a * 8 + b * 2 + c
+
+    sibling = col_of(z_lo, y, 1 - core)
+    partner = col_of(1 - z_lo, y, core)
+    y_cols = [col_of(z_lo, lax.rem(y + d, 4), core) for d in (1, 2, 3)]
+    y_far = [col_of(1 - z_lo, lax.rem(y + d, 4), core) for d in (1, 2, 3)]
+    z_rows = [x * 4 + lax.rem(z_hi + d, 4) for d in (1, 2, 3)]
+    x_rows = [lax.rem(x + d, 4) * 4 + z_hi for d in (1, 2, 3)]
+
+    barrier = pltpu.get_barrier_semaphore()
+    for c in [sibling, partner] + y_cols:
+        pl.semaphore_signal(barrier, inc=1, device_id=(row, c), device_id_type=MESH)
+    for r in z_rows + x_rows:
+        pl.semaphore_signal(barrier, inc=1, device_id=(r, col), device_id_type=MESH)
+
+    @pl.when(row != col)
+    def _():
+        pl.semaphore_signal(barrier, inc=1, device_id=(col, row), device_id_type=MESH)
+
+    at = pl.ds(pl.multiple_of(lax.div(col, 4) * BLOCK, BLOCK), BLOCK)
+    mine = pl.ds(pl.multiple_of(lax.rem(col, 4) * width, width), width)
+    for c in (0, 1):
+        turn_ref[c] = across(locs_ref[c : c + 1, at])
+    for b in range(rows // BLOCK):
+        s = slice(b * BLOCK, (b + 1) * BLOCK)
+        value = exp_distance(turn_ref[0, mine, :] - row_locs_ref[0:1, s], turn_ref[1, mine, :] - row_locs_ref[1:2, s])
+        part_ref[:, s] = value - prior_ref[:, s]
+
+    pl.semaphore_wait(barrier, jnp.where(row == col, 11, 12))
+
+    def slice_of(c):
+        return panel_ref.at[pl.ds(pl.multiple_of(c * width, width), width), :]
+
+    def piece_of(r):
+        return tile_ref.at[pl.ds(pl.multiple_of(r * width, width), width), :]
+
+    def send(src, dst, send_sem, recv_sem, to):
+        pltpu.make_async_remote_copy(src_ref=src, dst_ref=dst, send_sem=send_sem, recv_sem=recv_sem, device_id=to, device_id_type=MESH).start()
+
+    def send_slice(src, c, slot, to_col):
+        send(src, slice_of(c), panel_send.at[slot], panel_recv.at[c], (row, to_col))
+
+    def send_piece(r, slot, to_row):
+        send(piece_of(r), piece_of(r), tile_send.at[slot], tile_recv.at[r], (to_row, col))
+
+    def arrived(ref, sem):
+        pltpu.make_async_copy(ref, ref, sem).wait()
+
+    own_copy = pltpu.make_async_copy(part_ref, slice_of(col), own_sem)
+    swap_src = part_ref.at[:, 0:tile]
+    locs_src = row_locs_ref.at[:, 0:tile]
+    swap_copy = pltpu.make_async_remote_copy(src_ref=swap_src, dst_ref=piece_of(col), send_sem=swap_send.at[0], recv_sem=tile_recv.at[col], device_id=(col, row), device_id_type=MESH)
+    locs_copy = pltpu.make_async_remote_copy(src_ref=locs_src, dst_ref=col_locs_ref, send_sem=swap_send.at[1], recv_sem=locs_recv, device_id=(col, row), device_id_type=MESH)
+
+    send_slice(part_ref, col, 0, partner)
+
+    @pl.when(row != col)
+    def _():
+        swap_copy.start()
+        locs_copy.start()
+
+    @pl.when(row == col)
+    def _():
+        pltpu.make_async_copy(swap_src, piece_of(row), tile_recv.at[row]).start()
+        pltpu.make_async_copy(locs_src, col_locs_ref, locs_recv).start()
+
+    for j in range(3):
+        send_slice(part_ref, col, 1 + j, y_cols[j])
+    send_slice(part_ref, col, 4, sibling)
+    own_copy.start()
+
+    fill_matrix(locs_ref, m_ref, n)
+
+    def one_block(k, carry):
+        invert_step(k, blocks, m_ref, d_ref, inv_ref)
+
+        @pl.when(k == 0)
+        def _():
+            arrived(slice_of(partner), panel_recv.at[partner])
+            for j in range(3):
+                send_slice(slice_of(partner), partner, 5 + j, y_cols[j])
+            send_slice(slice_of(partner), partner, 8, sibling)
+            arrived(piece_of(row), tile_recv.at[row])
+            for j in range(3):
+                send_piece(row, j, z_rows[j])
+                send_piece(row, 3 + j, x_rows[j])
+
+        @pl.when(k == 1)
+        def _():
+            for j in range(3):
+                arrived(piece_of(z_rows[j]), tile_recv.at[z_rows[j]])
+                for i in range(3):
+                    send_piece(z_rows[j], 6 + 3 * j + i, x_rows[i])
+
+        @pl.when(k == 2)
+        def _():
+            for j in range(3):
+                arrived(slice_of(y_cols[j]), panel_recv.at[y_cols[j]])
+                send_slice(slice_of(y_cols[j]), y_cols[j], 9 + j, sibling)
+
+        return carry
+
+    lax.fori_loop(0, blocks, one_block, 0)
+
+    for j in range(3):
+        arrived(slice_of(y_far[j]), panel_recv.at[y_far[j]])
+        send_slice(slice_of(y_far[j]), y_far[j], 12 + j, sibling)
+
+    for a in range(2):
+        for b in range(4):
+            c = col_of(a, b, 1 - core)
+            arrived(slice_of(c), panel_recv.at[c])
+    for d in (1, 2, 3):
+        for e in range(4):
+            r = lax.rem(x + d, 4) * 4 + e
+            arrived(piece_of(r), tile_recv.at[r])
+    arrived(col_locs_ref, locs_recv)
+    own_copy.wait()
+    for slot in range(15):
+        arrived(slice_of(col), panel_send.at[slot])
+        arrived(piece_of(row), tile_send.at[slot])
+
+    @pl.when(row != col)
+    def _():
+        swap_copy.wait_send()
+        locs_copy.wait_send()
+
+
+def gather_and_invert(panel_locs, row_locs, prior_t, tile):
+    n = panel_locs.shape[1]
+    width, rows = prior_t.shape
+    n_col = n // width
+    vmem = pl.BlockSpec(memory_space=pltpu.VMEM)
+    anywhere = pl.BlockSpec(memory_space=pl.ANY)
+    dma = pltpu.SemaphoreType.DMA
+    return pl.pallas_call(
+        gather_kernel,
+        out_shape=(
+            jax.ShapeDtypeStruct((n, rows), f32),
+            jax.ShapeDtypeStruct((n, tile), f32),
+            jax.ShapeDtypeStruct((n, n), f32),
+            jax.ShapeDtypeStruct((2, tile), f32),
+        ),
+        in_specs=[vmem] * 3,
+        out_specs=(anywhere, anywhere, vmem, vmem),
+        scratch_shapes=[
+            pltpu.VMEM((n, n), f32),
+            pltpu.VMEM((BLOCK, BLOCK), f32),
+            pltpu.VMEM((width, rows), f32),
+            pltpu.VMEM((2, BLOCK, BLOCK), f32),
+            dma((15,)), dma((n_col,)), dma((15,)), dma((n_col,)), dma((2,)), dma, dma,
+        ],
+        compiler_params=pltpu.CompilerParams(vmem_limit_bytes=VMEM_A, collective_id=0, has_side_effects=True),
+        cost_estimate=pl.CostEstimate(flops=2 * n**3, bytes_accessed=8 * n * n, transcendentals=n * n),
+        name="gather_and_invert",
+    )(panel_locs, row_locs, prior_t)
 
 
 def body(row_locs, panel_locs, prior_panel, prior_trail):
     tile = panel_locs.shape[1]
-    width = prior_panel.shape[1]
-    n = lax.axis_size("col")
-    my_panel_locs = lax.dynamic_slice_in_dim(panel_locs, lax.axis_index("col") * width, width, 1)
-    part = covariance(my_panel_locs, row_locs) - prior_panel.T
-    swap = [(r * n + c, c * n + r) for r in range(n) for c in range(n)]
-    packed = jnp.concatenate([part[:, :tile], row_locs[:, :tile], jnp.zeros((6, tile), f32)], axis=0)
-    packed = lax.ppermute(packed, ("row", "col"), swap)
-    tile_t = lax.all_gather(packed[:width], "row", axis=0, tiled=True)
-    panel_t = lax.all_gather(part, "col", axis=0, tiled=True)
-    inv_lower = invert_factor(panel_locs)
-    return trailing_update(panel_t, tile_t, inv_lower, row_locs, packed[width : width + 2], prior_trail)
+    panel_t, tile_t, inv_lower, col_locs = gather_and_invert(panel_locs, row_locs, prior_panel.T, tile)
+    return trailing_update(panel_t, tile_t, inv_lower, row_locs, col_locs, prior_trail)
 
 
 def solution(mesh):

time: 146 us -> 58.8 us (0.40)
  the two profiles are of different devices: /device:TPU:1 before, /device:TPU:3 now
where the time goes in v1:
time: 58.8 us; the launch traced here: 58.5 us
  Pallas kernels  57.9 us (98%)
  between operations  0.64 us (1%)
    pallas_call x1, Pallas kernels, gather_and_invert(): pl.pallas_call(gather_kernel, out_shape=(jax.ShapeDtypeStruct((n, rows),...  43.4 us
    pallas_call x1, Pallas kernels, trailing_update(): pl.pallas_call(trailing_kernel, grid=(rows // ROW_TILE,), out_shape=(jax....  14.5 us

profile of v1, /device:TPU:3, one launch (start us, length us, event | category | flops | bytes accessed | tf_op | source)
XLA Modules:
  0.0 58.5 jit_solution(430655934862508488)
XLA Ops:
  0.6 43.4 %gather_and_invert.1 = (f32[512,2048]{1,0:T(8,128)}, f32[512,512]{1,0:T(8,128)}, f32[512,512]{1,0:T(8,128)}, f32[2,512]{1,0:T(2,128)}) custom-call(f32[2,512]{1,0:T(2,128)} %locs_ref.1, f32[2,2048]{1,0:T(2,128)} %row_locs_ref.3, f32[32,2048]{1,0:T(8,128)} %bitcast.1), custom_call_target="tpu_custom_call" | custom-call | flops 268435456 | bytes 2097152 | tf_op jit(solution)/shard_map/gather_and_invert/pallas_call | solution.py:345
  44.1 14.5 %trailing_update.1 = (f32[2048,512]{1,0:T(8,128)}, f32[2048,512]{1,0:T(8,128)}) custom-call(f32[512,2048]{1,0:T(8,128)} %get-tuple-element.6.panel_ref, f32[512,512]{1,0:T(8,128)} %get-tuple-element.7.tile_ref, f32[512,512]{1,0:T(8,128)} %get-tuple-element.8.inv_ref, f32[2,2048]{1,0:T(2,128)} %row_locs_ref.3, f32[2,512]{1,0:T(2,128)} %get-tuple-element.9.col_locs_ref, ...), custom_call_target="tpu_custom_call" | custom-call | flops 6442450944 | bytes 16777216 | tf_op jit(solution)/shard_map/trailing_update/pallas_call | solution.py:150

commit v2 on v1

v2 whole, which is shorter than its diff:
```python
import jax
import jax.numpy as jnp
from jax import lax
from jax.experimental import pallas as pl
from jax.experimental.pallas import tpu as pltpu
from jax.sharding import PartitionSpec as P

STRIP = 16
BLOCK = 128
VMEM_A = 24 * 2**20
VMEM_B = 24 * 2**20
f32, bf16 = jnp.float32, jnp.bfloat16


def exp_distance(dx, dy):
    d2 = dx * dx + dy * dy
    return jnp.exp(d2 * lax.rsqrt(jnp.maximum(d2, 1e-30)) * -10.0)


def split3(x):
    a = x.astype(bf16)
    r = x - a.astype(f32)
    b = r.astype(bf16)
    return a, b, (r - b.astype(f32)).astype(bf16)


def lanes_of(x, j):
    return jnp.broadcast_to(x[:, j : j + 1], (8, BLOCK))


def row_of(x, i):
    return jnp.broadcast_to(x[i : i + 1, :], (8, BLOCK))


def invert_block(d_ref, half_way):
    lane = lax.broadcasted_iota(jnp.int32, (8, BLOCK), 1)
    sub = lax.broadcasted_iota(jnp.int32, (8, BLOCK), 0)
    groups = STRIP // 8
    for strip in range(BLOCK // STRIP):
        base = strip * STRIP
        rows = [d_ref[base + 8 * g : base + 8 * g + 8, :] for g in range(groups)]
        cols = [[lanes_of(rows[g], base + j) for g in range(groups)] for j in range(STRIP)]
        scale = [jnp.zeros((8, BLOCK), f32)] * groups
        for i in range(STRIP):
            h, q = i // 8, i % 8
            pivot = row_of(cols[i][h], q)
            inv_pivot = 1.0 / pivot
            scale[h] = jnp.where(sub == q, lax.rsqrt(pivot), scale[h])
            f = [None] * groups
            f[h] = jnp.where(sub > q, cols[i][h], 0.0) * inv_pivot
            for g in range(h + 1, groups):
                f[g] = cols[i][g] * inv_pivot
            for j in range(i + 1, STRIP):
                t = row_of(cols[j][h], q)
                for g in range(h, groups):
                    cols[j][g] = cols[j][g] - f[g] * t
            rows[h] = jnp.where(lane == base + i, jnp.where(sub == q, 1.0, 0.0), rows[h])
            for g in range(h + 1, groups):
                rows[g] = jnp.where(lane == base + i, 0.0, rows[g])
            t = row_of(rows[h], q)
            for g in range(h, groups):
                rows[g] = rows[g] - f[g] * t
        for g in range(groups):
            above = (lane > base + 8 * g + sub) & (lane < base + STRIP)
            rows[g] = jnp.where(above, 0.0, rows[g]) * scale[g]
            d_ref[base + 8 * g : base + 8 * g + 8, :] = rows[g]
        first = base + STRIP
        if strip == 3:
            half_way()
        if first < BLOCK:
            a, b, c = split3(jnp.concatenate(rows, axis=0))
            left = jnp.concatenate([a, a, b, a, b, c], axis=0)
            right = jnp.concatenate([a, b, a, c, b, a], axis=0)
            update = lax.dot_general(left, right, (((0,), (0,)), ((), ())), preferred_element_type=f32)
            wide = lax.broadcasted_iota(jnp.int32, (BLOCK - first, BLOCK), 1)
            old = jnp.where((wide >= base) & (wide < first), 0.0, d_ref[first:, :])
            d_ref[first:, :] = old - update[first:, :]


def hdot(a, b, dims):
    return lax.dot_general(a, b, (dims, ((), ())), precision=lax.Precision.HIGHEST, preferred_element_type=f32)


def fill_matrix(locs_ref, m_ref, n):
    blocks = n // BLOCK
    eye = lax.broadcasted_iota(jnp.int32, (BLOCK, BLOCK), 0) == lax.broadcasted_iota(jnp.int32, (BLOCK, BLOCK), 1)
    for bi in range(blocks):
        col = [jnp.transpose(jnp.broadcast_to(locs_ref[c : c + 1, bi * BLOCK : (bi + 1) * BLOCK], (BLOCK, BLOCK))) for c in (0, 1)]
        for bj in range(blocks):
            at = (slice(bi * BLOCK, (bi + 1) * BLOCK), slice(bj * BLOCK, (bj + 1) * BLOCK))
            if bj < bi:
                m_ref[at] = jnp.zeros((BLOCK, BLOCK), f32)
                continue
            row = [locs_ref[c : c + 1, bj * BLOCK : (bj + 1) * BLOCK] for c in (0, 1)]
            value = exp_distance(col[0] - row[0], col[1] - row[1])
            if bi == bj:
                value = value + jnp.where(eye, 0.1, 0.0)
            m_ref[at] = value


ROW_TILE = 256


def split2(x):
    high = x.astype(bf16)
    return high, (x - high.astype(f32)).astype(bf16)


def dot3(left, right):
    def one(a, b):
        return lax.dot_general(a, b, (((1,), (1,)), ((), ())), preferred_element_type=f32)

    return one(left[0], right[0]) + (one(left[0], right[1]) + one(left[1], right[0]))


def across(row):
    return jnp.transpose(jnp.broadcast_to(row, (BLOCK, BLOCK)))


def trailing_kernel(panel_ref, tile_ref, inv_ref, gap_ref, factor_ref, out_ref, factor_buf, out_buf, col_h, col_l, inv_h, inv_l, sems):
    rows = panel_ref.shape[1]
    inv_h[...], inv_l[...] = split2(inv_ref[...])
    col_h[...], col_l[...] = split2(dot3(split2(jnp.transpose(tile_ref[...])), (inv_h[...], inv_l[...])))

    def out_copy(buf, ref, which, i):
        at = pl.ds(i * ROW_TILE, ROW_TILE)
        return pltpu.make_async_copy(buf.at[at, :], ref.at[at, :], sems.at[which, i])

    for i in range(rows // ROW_TILE):
        at = slice(i * ROW_TILE, (i + 1) * ROW_TILE)
        factor = dot3(split2(jnp.transpose(panel_ref[:, at])), (inv_h[...], inv_l[...]))
        factor_buf[at, :] = factor
        out_copy(factor_buf, factor_ref, 0, i).start()
        update = dot3(split2(factor), (col_h[...], col_l[...]))
        out_buf[at, :] = gap_ref[at, :] - update
        out_copy(out_buf, out_ref, 1, i).start()
    for i in range(rows // ROW_TILE):
        out_copy(factor_buf, factor_ref, 0, i).wait()
        out_copy(out_buf, out_ref, 1, i).wait()


def trailing_update(panel_t, tile_t, inv_lower, gap):
    depth, rows = panel_t.shape
    width = gap.shape[1]
    vmem = pl.BlockSpec(memory_space=pltpu.VMEM)
    anywhere = pl.BlockSpec(memory_space=pl.ANY)
    return pl.pallas_call(
        trailing_kernel,
        out_shape=(jax.ShapeDtypeStruct((rows, depth), f32), jax.ShapeDtypeStruct((rows, width), f32)),
        in_specs=[vmem] * 4,
        out_specs=(anywhere, anywhere),
        scratch_shapes=[
            pltpu.VMEM((rows, depth), f32),
            pltpu.VMEM((rows, width), f32),
            pltpu.VMEM((width, depth), bf16),
            pltpu.VMEM((width, depth), bf16),
            pltpu.VMEM((depth, depth), bf16),
            pltpu.VMEM((depth, depth), bf16),
            pltpu.SemaphoreType.DMA((2, rows // ROW_TILE)),
        ],
        compiler_params=pltpu.CompilerParams(vmem_limit_bytes=VMEM_B),
        cost_estimate=pl.CostEstimate(flops=12 * rows * depth * width, bytes_accessed=16 * rows * width, transcendentals=0),
        name="trailing_update",
    )(panel_t, tile_t, inv_lower, gap)


MESH = pl.DeviceIdType.MESH


def invert_step(k, blocks, m_ref, d_ref, inv_ref, hand_over):
    n = m_ref.shape[1]
    lower = lax.broadcasted_iota(jnp.int32, (BLOCK, BLOCK), 0) >= lax.broadcasted_iota(jnp.int32, (BLOCK, BLOCK), 1)
    lane_block = lax.broadcasted_iota(jnp.int32, (BLOCK, n), 1) // BLOCK
    mine = pl.ds(pl.multiple_of(k * BLOCK, BLOCK), BLOCK)
    d_ref[...] = m_ref[mine, mine]
    invert_block(d_ref, lambda: hand_over(0))
    w = jnp.where(lower, d_ref[...], 0.0)
    m_ref[mine, :] = hdot(w, m_ref[mine, :], ((1,), (0,)))
    m_ref[mine, mine] = w
    row = m_ref[mine, :]
    inv_ref[mine, :] = jnp.where(lane_block <= k, row, 0.0)

    def below(i, carry):
        his = pl.ds(pl.multiple_of(i * BLOCK, BLOCK), BLOCK)
        update = hdot(m_ref[mine, his], row, ((0,), (0,)))
        m_ref[his, :] = jnp.where(lane_block == k, 0.0, m_ref[his, :]) - update
        return carry

    hand_over(1)
    lax.fori_loop(k + 1, blocks, below, 0)


TRAIL_PARTS = 4


def trail_copy(trail_ref, trail_buf, trail_sems, part):
    size = trail_buf.shape[0] // TRAIL_PARTS
    at = pl.ds(part * size, size)
    return pltpu.make_async_copy(trail_ref.at[at, :], trail_buf.at[at, :], trail_sems.at[part])


def fill_gap(b, same, row_locs_ref, col_locs_ref, trail_buf, gap_ref):
    rows = pl.ds(pl.multiple_of(b * BLOCK, BLOCK), BLOCK)
    width = gap_ref.shape[1]
    xr, yr = across(row_locs_ref[0:1, rows]), across(row_locs_ref[1:2, rows])
    i = lax.broadcasted_iota(jnp.int32, (BLOCK, BLOCK), 0) + b * BLOCK
    for block in range(width // BLOCK):
        cols = slice(block * BLOCK, (block + 1) * BLOCK)
        value = exp_distance(xr - col_locs_ref[0:1, cols], yr - col_locs_ref[1:2, cols])
        j = lax.broadcasted_iota(jnp.int32, (BLOCK, BLOCK), 1) + block * BLOCK
        value = value + jnp.where((i == j) & same, 0.1, 0.0)
        gap_ref[rows, cols] = value - trail_buf[rows, cols]


def gather_kernel(
    locs_hbm, row_locs_hbm, prior_hbm, trail_ref,
    panel_ref, tile_ref, inv_ref, gap_ref,
    m_ref, d_ref, part_ref, turn_ref, trail_buf, col_locs_ref, locs_ref, row_locs_ref, prior_ref, trail_sems, in_sems,
    slice_send, slice_recv, piece_send, piece_recv, block_send, block_recv, swap_send, locs_recv, own_sem,
):
    n = locs_ref.shape[1]
    width, rows = prior_ref.shape
    tile = col_locs_ref.shape[1]
    blocks = n // BLOCK
    row, col = lax.axis_index("row"), lax.axis_index("col")
    x, z_hi = lax.div(row, 4), lax.rem(row, 4)
    z_lo, y, core = lax.div(col, 8), lax.rem(lax.div(col, 2), 4), lax.rem(col, 2)

    def near(i):
        return [lax.rem(i + d, 4) for d in (3, 1, 2)]

    def col_of(a, b, c):
        return a * 8 + b * 2 + c

    sibling = col_of(z_lo, y, 1 - core)
    partner = col_of(1 - z_lo, y, core)
    y_own = [col_of(z_lo, b, core) for b in near(y)]
    y_far = [col_of(1 - z_lo, b, core) for b in near(y)]
    z_rows = [x * 4 + b for b in near(z_hi)]
    x_near = near(x)
    x_rows = [b * 4 + z_hi for b in x_near]

    loads = [
        pltpu.make_async_copy(src, dst, in_sems.at[i])
        for i, (src, dst) in enumerate([(locs_hbm, locs_ref), (row_locs_hbm, row_locs_ref), (prior_hbm, prior_ref)])
    ]
    for copy in loads:
        copy.start()
    barrier = pltpu.get_barrier_semaphore()
    for b in range(TRAIL_PARTS):
        trail_copy(trail_ref, trail_buf, trail_sems, b).start()
    for c in [sibling, partner] + y_own[:2]:
        pl.semaphore_signal(barrier, inc=1, device_id=(row, c), device_id_type=MESH)
    for r in z_rows[:2] + x_rows[:2]:
        pl.semaphore_signal(barrier, inc=1, device_id=(r, col), device_id_type=MESH)

    @pl.when(row != col)
    def _():
        pl.semaphore_signal(barrier, inc=1, device_id=(col, row), device_id_type=MESH)

    for copy in loads:
        copy.wait()

    at = pl.ds(pl.multiple_of(lax.div(col, 4) * BLOCK, BLOCK), BLOCK)
    mine = pl.ds(pl.multiple_of(lax.rem(col, 4) * width, width), width)
    for c in (0, 1):
        turn_ref[c] = across(locs_ref[c : c + 1, at])
    for b in range(rows // BLOCK):
        s = slice(b * BLOCK, (b + 1) * BLOCK)
        value = exp_distance(turn_ref[0, mine, :] - row_locs_ref[0:1, s], turn_ref[1, mine, :] - row_locs_ref[1:2, s])
        part_ref[:, s] = value - prior_ref[:, s]

    pl.semaphore_wait(barrier, jnp.where(row == col, 8, 9))

    def cut(ref, index, size, half):
        if half is None:
            return ref.at[pl.ds(pl.multiple_of(index * size, size), size), :]
        return ref.at[pl.ds(pl.multiple_of(index * size + half * (size // 2), size // 2), size // 2), :]

    def slice_of(c, half=None):
        return cut(panel_ref, c, width, half)

    def piece_of(r, half=None):
        return cut(tile_ref, r, width, half)

    def block_of(b, half=None):
        return cut(tile_ref, b, 4 * width, half)

    sent = []

    def send(of, sends, recvs, index, half, to, src=None):
        slot = sum(1 for entry in sent if entry[1] is sends)
        sent.append((of, sends, slot, half))
        dst = of(index, half)
        pltpu.make_async_remote_copy(
            src_ref=dst if src is None else src,
            dst_ref=dst,
            send_sem=sends.at[slot],
            recv_sem=recvs.at[index, half or 0],
            device_id=to,
            device_id_type=MESH,
        ).start()

    def send_slice(c, to_col, half=None, src=None):
        send(slice_of, slice_send, slice_recv, c, half, (row, to_col), src)

    def send_piece(r, to_row, half=None):
        send(piece_of, piece_send, piece_recv, r, half, (to_row, col))

    def send_block(b, to_row, half=None):
        send(block_of, block_send, block_recv, b, half, (to_row, col))

    def wait_bytes(ref, sem):
        pltpu.make_async_copy(ref, ref, sem).wait()

    def arrived(of, recvs, index, half=None):
        wait_bytes(of(index, half), recvs.at[index, half or 0])

    own_copy = pltpu.make_async_copy(part_ref, slice_of(col), own_sem)
    swap_src = part_ref.at[:, 0:tile]
    locs_src = row_locs_ref.at[:, 0:tile]
    swap_copy = pltpu.make_async_remote_copy(src_ref=swap_src, dst_ref=piece_of(col), send_sem=swap_send.at[0], recv_sem=piece_recv.at[col, 0], device_id=(col, row), device_id_type=MESH)
    locs_copy = pltpu.make_async_remote_copy(src_ref=locs_src, dst_ref=col_locs_ref, send_sem=swap_send.at[1], recv_sem=locs_recv, device_id=(col, row), device_id_type=MESH)

    @pl.when(row != col)
    def _():
        swap_copy.start()
        locs_copy.start()

    @pl.when(row == col)
    def _():
        pltpu.make_async_copy(swap_src, piece_of(row), piece_recv.at[row, 0]).start()
        pltpu.make_async_copy(locs_src, col_locs_ref, locs_recv).start()

    send_slice(col, partner, src=part_ref)
    for c in y_own[:2]:
        send_slice(col, c, src=part_ref)
    send_slice(col, sibling, src=part_ref)
    own_copy.start()

    def tile_to_z():
        arrived(piece_of, piece_recv, row)
        for r in z_rows[:2]:
            send_piece(row, r)

    def partner_to_y():
        arrived(slice_of, slice_recv, partner)
        for c in y_own[:2]:
            send_slice(partner, c)
        send_slice(partner, sibling)

    def pass_on(sources, targets):
        for h in (0, 1):
            arrived(slice_of, slice_recv, sources[h])
            send_slice(sources[h], targets[1 - h], half=h)
            send_slice(sources[h], sibling)

    def opposite_slice(c):
        for h in (0, 1):
            arrived(slice_of, slice_recv, c, h)
        send_slice(c, sibling)

    def pieces_on():
        for h in (0, 1):
            arrived(piece_of, piece_recv, z_rows[h])
            send_piece(z_rows[h], z_rows[1 - h], half=h)

    def tile_to_x():
        for h in (0, 1):
            arrived(piece_of, piece_recv, z_rows[2], h)
        for r in x_rows[:2]:
            send_block(x, r)

    def blocks_on():
        for h in (0, 1):
            arrived(block_of, block_recv, x_near[h])
            send_block(x_near[h], x_rows[1 - h], half=h)

    stages = {
        0: [tile_to_z],
        1: [partner_to_y, lambda: pass_on(y_own, y_own)],
        2: [pieces_on],
        3: [tile_to_x],
        4: [lambda: pass_on(y_far, y_own)],
        5: [lambda: opposite_slice(y_own[2])],
        6: [blocks_on, lambda: opposite_slice(y_far[2])],
    }

    late = {}

    fill_matrix(locs_ref, m_ref, n)

    def one_block(k, carry):
        def hand_over(part):
            for stage in range(part, 2 * blocks, 2):
                if stage in stages:
                    @pl.when(k == stage // 2)
                    def _():
                        for task in stages[stage]:
                            task()

        invert_step(k, blocks, m_ref, d_ref, inv_ref, hand_over)
        return carry

    lax.fori_loop(0, blocks, one_block, 0)

    wait_bytes(col_locs_ref, locs_recv)
    for part in range(TRAIL_PARTS):
        trail_copy(trail_ref, trail_buf, trail_sems, part).wait()

    def one_gap(b, carry):
        fill_gap(b, row == col, row_locs_ref, col_locs_ref, trail_buf, gap_ref)
        for step, tasks in late.items():
            @pl.when(b == step)
            def _():
                for task in tasks:
                    task()
        return carry

    lax.fori_loop(0, rows // BLOCK, one_gap, 0)

    for a in range(2):
        for b in range(4):
            arrived(slice_of, slice_recv, col_of(a, b, 1 - core))
    for h in (0, 1):
        arrived(block_of, block_recv, x_near[2], h)
    own_copy.wait()
    for of, sends, slot, half in sent:
        wait_bytes(of(0, half), sends.at[slot])

    @pl.when(row != col)
    def _():
        swap_copy.wait_send()
        locs_copy.wait_send()


def gather_and_invert(panel_locs, row_locs, prior_t, prior_trail):
    n = panel_locs.shape[1]
    width, rows = prior_t.shape
    n_col = n // width
    tile = prior_trail.shape[1]
    vmem = pl.BlockSpec(memory_space=pltpu.VMEM)
    anywhere = pl.BlockSpec(memory_space=pl.ANY)
    dma = pltpu.SemaphoreType.DMA
    return pl.pallas_call(
        gather_kernel,
        out_shape=(
            jax.ShapeDtypeStruct((n, rows), f32),
            jax.ShapeDtypeStruct((n, tile), f32),
            jax.ShapeDtypeStruct((n, n), f32),
            jax.ShapeDtypeStruct((rows, tile), f32),
        ),
        in_specs=[pl.BlockSpec(memory_space=pltpu.HBM)] * 4,
        out_specs=(vmem, vmem, vmem, vmem),
        scratch_shapes=[
            pltpu.VMEM((n, n), f32),
            pltpu.VMEM((BLOCK, BLOCK), f32),
            pltpu.VMEM((width, rows), f32),
            pltpu.VMEM((2, BLOCK, BLOCK), f32),
            pltpu.VMEM((rows, tile), f32),
            pltpu.VMEM((2, tile), f32),
            pltpu.VMEM((2, n), f32),
            pltpu.VMEM((2, rows), f32),
            pltpu.VMEM((width, rows), f32),
            dma((TRAIL_PARTS,)),
            dma((3,)),
            dma((17,)), dma((n_col, 2)), dma((4,)), dma((n_col, 2)), dma((4,)), dma((4, 2)), dma((2,)), dma, dma,
        ],
        compiler_params=pltpu.CompilerParams(vmem_limit_bytes=VMEM_A, collective_id=0, has_side_effects=True),
        cost_estimate=pl.CostEstimate(flops=2 * n**3, bytes_accessed=8 * n * n, transcendentals=n * n),
        name="gather_and_invert",
    )(panel_locs, row_locs, prior_t, prior_trail)


def body(row_locs, panel_locs, prior_panel, prior_trail):
    inputs = [pltpu.with_memory_space_constraint(a, pltpu.HBM) for a in (panel_locs, row_locs, prior_panel.T, prior_trail)]
    return trailing_update(*gather_and_invert(*inputs))


def solution(mesh):
    in_specs = (P(None, "row"), P(), P("row", "col"), P("row", "col"))
    out_specs = (P("row", None), P("row", "col"))
    return jax.shard_map(body, mesh=mesh, in_specs=in_specs, out_specs=out_specs, check_vma=False)
```

time: 58.8 us -> 52.3 us (0.89)
  the two profiles are of different devices: /device:TPU:3 before, /device:TPU:1 now
where the time goes in v2:
time: 52.3 us; the launch traced here: 52.2 us
  Pallas kernels  51.6 us (99%)
  between operations  0.64 us (1%)
    pallas_call x1, Pallas kernels, gather_and_invert(): pl.pallas_call(gather_kernel, out_shape=(jax.ShapeDtypeStruct((n, rows),...  42.5 us
    pallas_call x1, Pallas kernels, trailing_update(): pl.pallas_call(trailing_kernel, out_shape=(jax.ShapeDtypeStruct((rows, de...  9.1 us

profile of v2, /device:TPU:1, one launch (start us, length us, event | category | flops | bytes accessed | tf_op | source)
XLA Modules:
  0.0 52.2 jit_solution(14287979540477630812)
XLA Ops:
  0.6 42.5 %gather_and_invert.1 = (f32[512,2048]{1,0:T(8,128)S(1)}, f32[512,512]{1,0:T(8,128)S(1)}, f32[512,512]{1,0:T(8,128)S(1)}, f32[2048,512]{1,0:T(8,128)S(1)}) custom-call(f32[2,512]{1,0:T(2,128)} %locs_hbm.1, f32[2,2048]{1,0:T(2,128)} %row_locs_hbm.1, f32[32,2048]{1,0:T(8,128)} %bitcast.1, f32[2048,512]{1,0:T(8,128)} %trail_ref.1), custom_call_target="tpu_custom_call" | custom-call | flops 268435456 | bytes 2097152 | tf_op jit(solution)/shard_map/gather_and_invert/pallas_call | solution.py:445
  43.1 9.1 %trailing_update.1 = (f32[2048,512]{1,0:T(8,128)}, f32[2048,512]{1,0:T(8,128)}) custom-call(f32[512,2048]{1,0:T(8,128)S(1)} %get-tuple-element.6.panel_ref, f32[512,512]{1,0:T(8,128)S(1)} %get-tuple-element.7.tile_ref, f32[512,512]{1,0:T(8,128)S(1)} %get-tuple-element.8.inv_ref, f32[2048,512]{1,0:T(8,128)S(1)} %get-tuple-element.9.gap_ref), custom_call_target="tpu_custom_call" | custom-call | flops 6442450944 | bytes 16777216 | tf_op jit(solution)/shard_map/trailing_update/pallas_call | solution.py:147

commit v3 on v2

--- a/solution.py
+++ b/solution.py
@@ -32,7 +32,7 @@
     return jnp.broadcast_to(x[i : i + 1, :], (8, BLOCK))
 
 
-def invert_block(d_ref, half_way):
+def invert_block(d_ref, k, hand_over, beside):
     lane = lax.broadcasted_iota(jnp.int32, (8, BLOCK), 1)
     sub = lax.broadcasted_iota(jnp.int32, (8, BLOCK), 0)
     groups = STRIP // 8
@@ -65,8 +65,8 @@
             rows[g] = jnp.where(above, 0.0, rows[g]) * scale[g]
             d_ref[base + 8 * g : base + 8 * g + 8, :] = rows[g]
         first = base + STRIP
-        if strip == 3:
-            half_way()
+        if beside is not None and strip in BESIDE:
+            beside(k, BESIDE.index(strip))
         if first < BLOCK:
             a, b, c = split3(jnp.concatenate(rows, axis=0))
             left = jnp.concatenate([a, a, b, a, b, c], axis=0)
@@ -75,6 +75,8 @@
             wide = lax.broadcasted_iota(jnp.int32, (BLOCK - first, BLOCK), 1)
             old = jnp.where((wide >= base) & (wide < first), 0.0, d_ref[first:, :])
             d_ref[first:, :] = old - update[first:, :]
+        if strip % 2:
+            hand_over(k, strip // 2)
 
 
 def hdot(a, b, dims):
@@ -117,10 +119,15 @@
     return jnp.transpose(jnp.broadcast_to(row, (BLOCK, BLOCK)))
 
 
-def trailing_kernel(panel_ref, tile_ref, inv_ref, gap_ref, factor_ref, out_ref, factor_buf, out_buf, col_h, col_l, inv_h, inv_l, sems):
+def trailing_kernel(panel_ref, tile_ref, inv_ref, gap_ref, factor_ref, out_ref, factor_buf, out_buf, tile_buf, col_h, col_l, inv_h, inv_l, sems):
     rows = panel_ref.shape[1]
     inv_h[...], inv_l[...] = split2(inv_ref[...])
-    col_h[...], col_l[...] = split2(dot3(split2(jnp.transpose(tile_ref[...])), (inv_h[...], inv_l[...])))
+    col = lax.axis_index("col")
+    piece = tile_ref.shape[0] // 16
+    for r in range(16):
+        at = pl.ds(pl.multiple_of(piece_column(r, col) * piece, piece), piece)
+        tile_buf[at, :] = tile_ref[r * piece : (r + 1) * piece, :]
+    col_h[...], col_l[...] = split2(dot3(split2(jnp.transpose(tile_buf[...])), (inv_h[...], inv_l[...])))
 
     def out_copy(buf, ref, which, i):
         at = pl.ds(i * ROW_TILE, ROW_TILE)
@@ -152,6 +159,7 @@
         scratch_shapes=[
             pltpu.VMEM((rows, depth), f32),
             pltpu.VMEM((rows, width), f32),
+            pltpu.VMEM((depth, width), f32),
             pltpu.VMEM((width, depth), bf16),
             pltpu.VMEM((width, depth), bf16),
             pltpu.VMEM((depth, depth), bf16),
@@ -167,13 +175,13 @@
 MESH = pl.DeviceIdType.MESH
 
 
-def invert_step(k, blocks, m_ref, d_ref, inv_ref, hand_over):
+def invert_step(k, blocks, m_ref, d_ref, inv_ref, hand_over, beside):
     n = m_ref.shape[1]
     lower = lax.broadcasted_iota(jnp.int32, (BLOCK, BLOCK), 0) >= lax.broadcasted_iota(jnp.int32, (BLOCK, BLOCK), 1)
     lane_block = lax.broadcasted_iota(jnp.int32, (BLOCK, n), 1) // BLOCK
     mine = pl.ds(pl.multiple_of(k * BLOCK, BLOCK), BLOCK)
     d_ref[...] = m_ref[mine, mine]
-    invert_block(d_ref, lambda: hand_over(0))
+    invert_block(d_ref, k, hand_over, beside)
     w = jnp.where(lower, d_ref[...], 0.0)
     m_ref[mine, :] = hdot(w, m_ref[mine, :], ((1,), (0,)))
     m_ref[mine, mine] = w
@@ -186,11 +194,12 @@
         m_ref[his, :] = jnp.where(lane_block == k, 0.0, m_ref[his, :]) - update
         return carry
 
-    hand_over(1)
     lax.fori_loop(k + 1, blocks, below, 0)
 
 
 TRAIL_PARTS = 4
+POINTS = 4
+BESIDE = (0, 1, 3, 4, 6, 7)
 
 
 def trail_copy(trail_ref, trail_buf, trail_sems, part):
@@ -212,11 +221,16 @@
         gap_ref[rows, cols] = value - trail_buf[rows, cols]
 
 
+def piece_column(row, col):
+    turn = lax.rem(row + 16 - col, 16)
+    return lax.rem(turn, 2) * 8 + lax.div(turn, 4) * 2 + lax.rem(lax.div(turn, 2), 2)
+
+
 def gather_kernel(
     locs_hbm, row_locs_hbm, prior_hbm, trail_ref,
     panel_ref, tile_ref, inv_ref, gap_ref,
     m_ref, d_ref, part_ref, turn_ref, trail_buf, col_locs_ref, locs_ref, row_locs_ref, prior_ref, trail_sems, in_sems,
-    slice_send, slice_recv, piece_send, piece_recv, block_send, block_recv, swap_send, locs_recv, own_sem,
+    slice_send, slice_recv, piece_send, piece_recv, pair_send, pair_recv, swap_send, locs_recv, own_sem,
 ):
     n = locs_ref.shape[1]
     width, rows = prior_ref.shape
@@ -239,6 +253,10 @@
     z_rows = [x * 4 + b for b in near(z_hi)]
     x_near = near(x)
     x_rows = [b * 4 + z_hi for b in x_near]
+
+    swap_to = (lax.rem(y * 4 + core * 2 + z_lo + row, 16), row)
+    swap_from = (col, piece_column(row, col))
+    alone = row + col == 0
 
     loads = [
         pltpu.make_async_copy(src, dst, in_sems.at[i])
@@ -254,9 +272,9 @@
     for r in z_rows[:2] + x_rows[:2]:
         pl.semaphore_signal(barrier, inc=1, device_id=(r, col), device_id_type=MESH)
 
-    @pl.when(row != col)
+    @pl.when(jnp.logical_not(alone))
     def _():
-        pl.semaphore_signal(barrier, inc=1, device_id=(col, row), device_id_type=MESH)
+        pl.semaphore_signal(barrier, inc=1, device_id=swap_from, device_id_type=MESH)
 
     for copy in loads:
         copy.wait()
@@ -265,12 +283,14 @@
     mine = pl.ds(pl.multiple_of(lax.rem(col, 4) * width, width), width)
     for c in (0, 1):
         turn_ref[c] = across(locs_ref[c : c + 1, at])
-    for b in range(rows // BLOCK):
-        s = slice(b * BLOCK, (b + 1) * BLOCK)
-        value = exp_distance(turn_ref[0, mine, :] - row_locs_ref[0:1, s], turn_ref[1, mine, :] - row_locs_ref[1:2, s])
-        part_ref[:, s] = value - prior_ref[:, s]
-
-    pl.semaphore_wait(barrier, jnp.where(row == col, 8, 9))
+    def fill_part(first, last):
+        for b in range(first // BLOCK, last // BLOCK):
+            s = slice(b * BLOCK, (b + 1) * BLOCK)
+            value = exp_distance(turn_ref[0, mine, :] - row_locs_ref[0:1, s], turn_ref[1, mine, :] - row_locs_ref[1:2, s])
+            part_ref[:, s] = value - prior_ref[:, s]
+
+    fill_part(0, tile)
+    pl.semaphore_wait(barrier, jnp.where(alone, 8, 9))
 
     def cut(ref, index, size, half):
         if half is None:
@@ -282,9 +302,6 @@
 
     def piece_of(r, half=None):
         return cut(tile_ref, r, width, half)
-
-    def block_of(b, half=None):
-        return cut(tile_ref, b, 4 * width, half)
 
     sent = []
 
@@ -307,9 +324,6 @@
     def send_piece(r, to_row, half=None):
         send(piece_of, piece_send, piece_recv, r, half, (to_row, col))
 
-    def send_block(b, to_row, half=None):
-        send(block_of, block_send, block_recv, b, half, (to_row, col))
-
     def wait_bytes(ref, sem):
         pltpu.make_async_copy(ref, ref, sem).wait()
 
@@ -319,40 +333,48 @@
     own_copy = pltpu.make_async_copy(part_ref, slice_of(col), own_sem)
     swap_src = part_ref.at[:, 0:tile]
     locs_src = row_locs_ref.at[:, 0:tile]
-    swap_copy = pltpu.make_async_remote_copy(src_ref=swap_src, dst_ref=piece_of(col), send_sem=swap_send.at[0], recv_sem=piece_recv.at[col, 0], device_id=(col, row), device_id_type=MESH)
-    locs_copy = pltpu.make_async_remote_copy(src_ref=locs_src, dst_ref=col_locs_ref, send_sem=swap_send.at[1], recv_sem=locs_recv, device_id=(col, row), device_id_type=MESH)
-
-    @pl.when(row != col)
+    swap_copy = pltpu.make_async_remote_copy(src_ref=swap_src, dst_ref=piece_of(swap_to[0]), send_sem=swap_send.at[0], recv_sem=piece_recv.at[swap_to[0], 0], device_id=swap_to, device_id_type=MESH)
+    locs_copy = pltpu.make_async_remote_copy(src_ref=locs_src, dst_ref=col_locs_ref, send_sem=swap_send.at[1], recv_sem=locs_recv, device_id=swap_to, device_id_type=MESH)
+
+    @pl.when(jnp.logical_not(alone))
     def _():
         swap_copy.start()
         locs_copy.start()
 
-    @pl.when(row == col)
+    @pl.when(alone)
     def _():
         pltpu.make_async_copy(swap_src, piece_of(row), piece_recv.at[row, 0]).start()
         pltpu.make_async_copy(locs_src, col_locs_ref, locs_recv).start()
 
+    fill_part(tile, rows)
     send_slice(col, partner, src=part_ref)
-    for c in y_own[:2]:
-        send_slice(col, c, src=part_ref)
+    half_rows = [part_ref.at[pl.ds(h * (width // 2), width // 2), :] for h in (0, 1)]
+    for h in (0, 1):
+        send_slice(col, y_own[1], half=h, src=half_rows[h])
+        send_slice(col, y_own[0], half=1 - h, src=half_rows[1 - h])
     send_slice(col, sibling, src=part_ref)
     own_copy.start()
 
-    def tile_to_z():
+    def tile_on():
         arrived(piece_of, piece_recv, row)
-        for r in z_rows[:2]:
+        for r in z_rows[:2] + x_rows[:2]:
             send_piece(row, r)
 
     def partner_to_y():
         arrived(slice_of, slice_recv, partner)
-        for c in y_own[:2]:
-            send_slice(partner, c)
+        for h in (0, 1):
+            send_slice(partner, y_own[1], half=h)
+            send_slice(partner, y_own[0], half=1 - h)
         send_slice(partner, sibling)
 
-    def pass_on(sources, targets):
-        for h in (0, 1):
-            arrived(slice_of, slice_recv, sources[h])
-            send_slice(sources[h], targets[1 - h], half=h)
+    def pass_on(sources):
+        for h in (0, 1):
+            arrived(slice_of, slice_recv, sources[h], h)
+            send_slice(sources[h], y_own[1 - h], half=h)
+
+    def to_sibling(sources):
+        for h in (0, 1):
+            arrived(slice_of, slice_recv, sources[h], 1 - h)
             send_slice(sources[h], sibling)
 
     def opposite_slice(c):
@@ -364,71 +386,84 @@
         for h in (0, 1):
             arrived(piece_of, piece_recv, z_rows[h])
             send_piece(z_rows[h], z_rows[1 - h], half=h)
-
-    def tile_to_x():
+            for r in x_rows[:2]:
+                send_piece(z_rows[h], r)
+
+    def opposite_piece():
         for h in (0, 1):
             arrived(piece_of, piece_recv, z_rows[2], h)
         for r in x_rows[:2]:
-            send_block(x, r)
-
-    def blocks_on():
-        for h in (0, 1):
-            arrived(block_of, block_recv, x_near[h])
-            send_block(x_near[h], x_rows[1 - h], half=h)
-
-    stages = {
-        0: [tile_to_z],
-        1: [partner_to_y, lambda: pass_on(y_own, y_own)],
-        2: [pieces_on],
-        3: [tile_to_x],
-        4: [lambda: pass_on(y_far, y_own)],
-        5: [lambda: opposite_slice(y_own[2])],
-        6: [blocks_on, lambda: opposite_slice(y_far[2])],
-    }
-
-    late = {}
+            send_piece(z_rows[2], r)
+
+    def pair_of(b, half):
+        return cut(tile_ref, b, 4 * width, half)
+
+    def tiles_on():
+        for h in (0, 1):
+            for e in range(4):
+                arrived(piece_of, piece_recv, x_near[h] * 4 + e)
+            send(pair_of, pair_send, pair_recv, x_near[h], h, (x_rows[1 - h], col))
+
+    schedule = [(2, "own"), (3, "tile_on"), (4, "partner_to_y"), (4, "own_over"), (7, "pieces_on"), (7, "opposite_own"), (9, "opposite_piece"), (9, "far"), (11, "far_over"), (11, "tiles_on"), (13, "opposite_far")]
+    tasks = dict(
+        tile_on=tile_on,
+        partner_to_y=partner_to_y,
+        own=lambda: pass_on(y_own),
+        own_over=lambda: to_sibling(y_own),
+        far=lambda: pass_on(y_far),
+        far_over=lambda: to_sibling(y_far),
+        opposite_own=lambda: opposite_slice(y_own[2]),
+        opposite_far=lambda: opposite_slice(y_far[2]),
+        pieces_on=pieces_on,
+        opposite_piece=opposite_piece,
+        tiles_on=tiles_on,
+    )
+    stages = {}
+    for stage, name in schedule:
+        stages.setdefault(stage, []).append(tasks[name])
 
     fill_matrix(locs_ref, m_ref, n)
 
-    def one_block(k, carry):
-        def hand_over(part):
-            for stage in range(part, 2 * blocks, 2):
+    def hand_over(first, last):
+        def at_strip(k, part):
+            for stage in range(first * POINTS + part, last * POINTS, POINTS):
                 if stage in stages:
-                    @pl.when(k == stage // 2)
+                    @pl.when(k == stage // POINTS)
                     def _():
                         for task in stages[stage]:
                             task()
 
-        invert_step(k, blocks, m_ref, d_ref, inv_ref, hand_over)
-        return carry
-
-    lax.fori_loop(0, blocks, one_block, 0)
-
+        return at_strip
+
+    def beside(k, place):
+        b = jnp.minimum((k - 1) * len(BESIDE) + place, rows // BLOCK - 1)
+        fill_gap(b, row == col, row_locs_ref, col_locs_ref, trail_buf, gap_ref)
+
+    invert_step(0, blocks, m_ref, d_ref, inv_ref, hand_over(0, 1), None)
     wait_bytes(col_locs_ref, locs_recv)
     for part in range(TRAIL_PARTS):
         trail_copy(trail_ref, trail_buf, trail_sems, part).wait()
 
-    def one_gap(b, carry):
-        fill_gap(b, row == col, row_locs_ref, col_locs_ref, trail_buf, gap_ref)
-        for step, tasks in late.items():
-            @pl.when(b == step)
-            def _():
-                for task in tasks:
-                    task()
+    def one_block(k, carry):
+        invert_step(k, blocks, m_ref, d_ref, inv_ref, hand_over(1, blocks), beside)
         return carry
 
-    lax.fori_loop(0, rows // BLOCK, one_gap, 0)
+    lax.fori_loop(1, blocks, one_block, 0)
+    for stage in sorted(stages):
+        if stage >= POINTS * blocks:
+            for task in stages[stage]:
+                task()
 
     for a in range(2):
         for b in range(4):
             arrived(slice_of, slice_recv, col_of(a, b, 1 - core))
     for h in (0, 1):
-        arrived(block_of, block_recv, x_near[2], h)
+        wait_bytes(pair_of(x_near[2], h), pair_recv.at[x_near[2], h])
     own_copy.wait()
     for of, sends, slot, half in sent:
         wait_bytes(of(0, half), sends.at[slot])
 
-    @pl.when(row != col)
+    @pl.when(jnp.logical_not(alone))
     def _():
         swap_copy.wait_send()
         locs_copy.wait_send()
@@ -464,7 +499,7 @@
             pltpu.VMEM((width, rows), f32),
             dma((TRAIL_PARTS,)),
             dma((3,)),
-            dma((17,)), dma((n_col, 2)), dma((4,)), dma((n_col, 2)), dma((4,)), dma((4, 2)), dma((2,)), dma, dma,
+            dma((21,)), dma((n_col, 2)), dma((12,)), dma((n_col, 2)), dma((2,)), dma((4, 2)), dma((2,)), dma, dma,
         ],
         compiler_params=pltpu.CompilerParams(vmem_limit_bytes=VMEM_A, collective_id=0, has_side_effects=True),
         cost_estimate=pl.CostEstimate(flops=2 * n**3, bytes_accessed=8 * n * n, transcendentals=n * n),

time: 52.3 us -> 48 us (0.918)
  Pallas kernels: 51.6 us -> 47.1 us
    pallas_call x1, Pallas kernels: 42.5 us -> 37.9 us  [gather_and_invert(): pl.pallas_call(gather_kernel, out_shape=(jax.ShapeDtypeStruct((n, rows),...]
where the time goes in v3:
time: 48 us; the launch traced here: 47.9 us
  Pallas kernels  47.1 us (98%)
  between operations  0.8 us (2%)
    pallas_call x1, Pallas kernels, gather_and_invert(): pl.pallas_call(gather_kernel, out_shape=(jax.ShapeDtypeStruct((n, rows),...  37.9 us
    pallas_call x1, Pallas kernels, trailing_update(): pl.pallas_call(trailing_kernel, out_shape=(jax.ShapeDtypeStruct((rows, de...  9.25 us

profile of v3, /device:TPU:1, one launch (start us, length us, event | category | flops | bytes accessed | tf_op | source)
XLA Modules:
  0.0 47.9 jit_solution(5848235249227881564)
XLA Ops:
  0.6 37.9 %gather_and_invert.1 = (f32[512,2048]{1,0:T(8,128)S(1)}, f32[512,512]{1,0:T(8,128)S(1)}, f32[512,512]{1,0:T(8,128)S(1)}, f32[2048,512]{1,0:T(8,128)S(1)}) custom-call(f32[2,512]{1,0:T(2,128)} %locs_hbm.1, f32[2,2048]{1,0:T(2,128)} %row_locs_hbm.1, f32[32,2048]{1,0:T(8,128)} %bitcast.1, f32[2048,512]{1,0:T(8,128)} %trail_ref.1), custom_call_target="tpu_custom_call" | custom-call | flops 268435456 | bytes 2097152 | tf_op jit(solution)/shard_map/gather_and_invert/pallas_call | solution.py:480
  38.5 9.2 %trailing_update.1 = (f32[2048,512]{1,0:T(8,128)}, f32[2048,512]{1,0:T(8,128)}) custom-call(f32[512,2048]{1,0:T(8,128)S(1)} %get-tuple-element.6.panel_ref, f32[512,512]{1,0:T(8,128)S(1)} %get-tuple-element.7.tile_ref, f32[512,512]{1,0:T(8,128)S(1)} %get-tuple-element.8.inv_ref, f32[2048,512]{1,0:T(8,128)S(1)} %get-tuple-element.9.gap_ref), custom_call_target="tpu_custom_call" | custom-call | flops 6442450944 | bytes 16777216 | tf_op jit(solution)/shard_map/trailing_update/pallas_call | solution.py:154

commit v4 on v3

--- a/solution.py
+++ b/solution.py
@@ -6,6 +6,8 @@
 from jax.sharding import PartitionSpec as P
 
 STRIP = 16
+AHEAD = 2
+HAND_OVER = 2
 BLOCK = 128
 VMEM_A = 24 * 2**20
 VMEM_B = 24 * 2**20
@@ -35,12 +37,13 @@
 def invert_block(d_ref, k, hand_over, beside):
     lane = lax.broadcasted_iota(jnp.int32, (8, BLOCK), 1)
     sub = lax.broadcasted_iota(jnp.int32, (8, BLOCK), 0)
-    groups = STRIP // 8
+    own = STRIP // 8
     for strip in range(BLOCK // STRIP):
         base = strip * STRIP
+        groups = min(own + AHEAD, (BLOCK - base) // 8)
         rows = [d_ref[base + 8 * g : base + 8 * g + 8, :] for g in range(groups)]
         cols = [[lanes_of(rows[g], base + j) for g in range(groups)] for j in range(STRIP)]
-        scale = [jnp.zeros((8, BLOCK), f32)] * groups
+        scale = [jnp.zeros((8, BLOCK), f32)] * own
         for i in range(STRIP):
             h, q = i // 8, i % 8
             pivot = row_of(cols[i][h], q)
@@ -60,44 +63,44 @@
             t = row_of(rows[h], q)
             for g in range(h, groups):
                 rows[g] = rows[g] - f[g] * t
-        for g in range(groups):
+        for g in range(own):
             above = (lane > base + 8 * g + sub) & (lane < base + STRIP)
             rows[g] = jnp.where(above, 0.0, rows[g]) * scale[g]
+        for g in range(groups):
             d_ref[base + 8 * g : base + 8 * g + 8, :] = rows[g]
-        first = base + STRIP
         if beside is not None and strip in BESIDE:
             beside(k, BESIDE.index(strip))
+        first = base + 8 * groups
         if first < BLOCK:
-            a, b, c = split3(jnp.concatenate(rows, axis=0))
+            a, b, c = split3(jnp.concatenate(rows[:own], axis=0))
             left = jnp.concatenate([a, a, b, a, b, c], axis=0)
             right = jnp.concatenate([a, b, a, c, b, a], axis=0)
             update = lax.dot_general(left, right, (((0,), (0,)), ((), ())), preferred_element_type=f32)
             wide = lax.broadcasted_iota(jnp.int32, (BLOCK - first, BLOCK), 1)
-            old = jnp.where((wide >= base) & (wide < first), 0.0, d_ref[first:, :])
+            old = jnp.where((wide >= base) & (wide < base + STRIP), 0.0, d_ref[first:, :])
             d_ref[first:, :] = old - update[first:, :]
-        if strip % 2:
-            hand_over(k, strip // 2)
+        if strip % HAND_OVER == HAND_OVER - 1:
+            hand_over(k, strip // HAND_OVER)
 
 
 def hdot(a, b, dims):
     return lax.dot_general(a, b, (dims, ((), ())), precision=lax.Precision.HIGHEST, preferred_element_type=f32)
 
 
-def fill_matrix(locs_ref, m_ref, n):
+def fill_matrix(locs_ref, m_ref, n, bi):
     blocks = n // BLOCK
     eye = lax.broadcasted_iota(jnp.int32, (BLOCK, BLOCK), 0) == lax.broadcasted_iota(jnp.int32, (BLOCK, BLOCK), 1)
-    for bi in range(blocks):
-        col = [jnp.transpose(jnp.broadcast_to(locs_ref[c : c + 1, bi * BLOCK : (bi + 1) * BLOCK], (BLOCK, BLOCK))) for c in (0, 1)]
-        for bj in range(blocks):
-            at = (slice(bi * BLOCK, (bi + 1) * BLOCK), slice(bj * BLOCK, (bj + 1) * BLOCK))
-            if bj < bi:
-                m_ref[at] = jnp.zeros((BLOCK, BLOCK), f32)
-                continue
-            row = [locs_ref[c : c + 1, bj * BLOCK : (bj + 1) * BLOCK] for c in (0, 1)]
-            value = exp_distance(col[0] - row[0], col[1] - row[1])
-            if bi == bj:
-                value = value + jnp.where(eye, 0.1, 0.0)
-            m_ref[at] = value
+    col = [jnp.transpose(jnp.broadcast_to(locs_ref[c : c + 1, bi * BLOCK : (bi + 1) * BLOCK], (BLOCK, BLOCK))) for c in (0, 1)]
+    for bj in range(blocks):
+        at = (slice(bi * BLOCK, (bi + 1) * BLOCK), slice(bj * BLOCK, (bj + 1) * BLOCK))
+        if bj < bi:
+            m_ref[at] = jnp.zeros((BLOCK, BLOCK), f32)
+            continue
+        row = [locs_ref[c : c + 1, bj * BLOCK : (bj + 1) * BLOCK] for c in (0, 1)]
+        value = exp_distance(col[0] - row[0], col[1] - row[1])
+        if bi == bj:
+            value = value + jnp.where(eye, 0.1, 0.0)
+        m_ref[at] = value
 
 
 ROW_TILE = 256
@@ -117,6 +120,14 @@
 
 def across(row):
     return jnp.transpose(jnp.broadcast_to(row, (BLOCK, BLOCK)))
+
+
+def times_lower(left, inv_h, inv_l):
+    half = inv_h.shape[0] // 2
+    high, low = split2(left)
+    top = dot3((high[:, :half], low[:, :half]), (inv_h[:half, :half], inv_l[:half, :half]))
+    bottom = dot3((high, low), (inv_h[half:, :], inv_l[half:, :]))
+    return jnp.concatenate([top, bottom], axis=1)
 
 
 def trailing_kernel(panel_ref, tile_ref, inv_ref, gap_ref, factor_ref, out_ref, factor_buf, out_buf, tile_buf, col_h, col_l, inv_h, inv_l, sems):
@@ -127,7 +138,7 @@
     for r in range(16):
         at = pl.ds(pl.multiple_of(piece_column(r, col) * piece, piece), piece)
         tile_buf[at, :] = tile_ref[r * piece : (r + 1) * piece, :]
-    col_h[...], col_l[...] = split2(dot3(split2(jnp.transpose(tile_buf[...])), (inv_h[...], inv_l[...])))
+    col_h[...], col_l[...] = split2(times_lower(jnp.transpose(tile_buf[...]), inv_h, inv_l))
 
     def out_copy(buf, ref, which, i):
         at = pl.ds(i * ROW_TILE, ROW_TILE)
@@ -135,7 +146,7 @@
 
     for i in range(rows // ROW_TILE):
         at = slice(i * ROW_TILE, (i + 1) * ROW_TILE)
-        factor = dot3(split2(jnp.transpose(panel_ref[:, at])), (inv_h[...], inv_l[...]))
+        factor = times_lower(jnp.transpose(panel_ref[:, at]), inv_h, inv_l)
         factor_buf[at, :] = factor
         out_copy(factor_buf, factor_ref, 0, i).start()
         update = dot3(split2(factor), (col_h[...], col_l[...]))
@@ -198,7 +209,7 @@
 
 
 TRAIL_PARTS = 4
-POINTS = 4
+POINTS = BLOCK // STRIP // HAND_OVER
 BESIDE = (0, 1, 3, 4, 6, 7)
 
 
@@ -404,7 +415,7 @@
                 arrived(piece_of, piece_recv, x_near[h] * 4 + e)
             send(pair_of, pair_send, pair_recv, x_near[h], h, (x_rows[1 - h], col))
 
-    schedule = [(2, "own"), (3, "tile_on"), (4, "partner_to_y"), (4, "own_over"), (7, "pieces_on"), (7, "opposite_own"), (9, "opposite_piece"), (9, "far"), (11, "far_over"), (11, "tiles_on"), (13, "opposite_far")]
+    schedule = [(3, "own"), (4, "tile_on"), (5, "partner_to_y"), (6, "own_over"), (8, "pieces_on"), (8, "opposite_own"), (10, "far"), (11, "opposite_piece"), (12, "far_over"), (13, "tiles_on"), (15, "opposite_far")]
     tasks = dict(
         tile_on=tile_on,
         partner_to_y=partner_to_y,
@@ -422,7 +433,7 @@
     for stage, name in schedule:
         stages.setdefault(stage, []).append(tasks[name])
 
-    fill_matrix(locs_ref, m_ref, n)
+    fill_matrix(locs_ref, m_ref, n, 0)
 
     def hand_over(first, last):
         def at_strip(k, part):
@@ -439,7 +450,11 @@
         b = jnp.minimum((k - 1) * len(BESIDE) + place, rows // BLOCK - 1)
         fill_gap(b, row == col, row_locs_ref, col_locs_ref, trail_buf, gap_ref)
 
-    invert_step(0, blocks, m_ref, d_ref, inv_ref, hand_over(0, 1), None)
+    def fill_beside(k, place):
+        if place + 1 < blocks:
+            fill_matrix(locs_ref, m_ref, n, place + 1)
+
+    invert_step(0, blocks, m_ref, d_ref, inv_ref, hand_over(0, 1), fill_beside)
     wait_bytes(col_locs_ref, locs_recv)
     for part in range(TRAIL_PARTS):
         trail_copy(trail_ref, trail_buf, trail_sems, part).wait()

time: 48 us -> 46.2 us (0.963)
  Pallas kernels: 47.1 us -> 45.3 us
    pallas_call x1, Pallas kernels: 9.25 us -> 8.14 us  [trailing_update(): pl.pallas_call(trailing_kernel, out_shape=(jax.ShapeDtypeStruct((rows, de...]
    pallas_call x1, Pallas kernels: 37.9 us -> 37.1 us  [gather_and_invert(): pl.pallas_call(gather_kernel, out_shape=(jax.ShapeDtypeStruct((n, rows),...]
where the time goes in v4:
time: 46.2 us; the launch traced here: 46.1 us
  Pallas kernels  45.3 us (98%)
  between operations  0.8 us (2%)
    pallas_call x1, Pallas kernels, gather_and_invert(): pl.pallas_call(gather_kernel, out_shape=(jax.ShapeDtypeStruct((n, rows),...  37.1 us
    pallas_call x1, Pallas kernels, trailing_update(): pl.pallas_call(trailing_kernel, out_shape=(jax.ShapeDtypeStruct((rows, de...  8.14 us

profile of v4, /device:TPU:1, one launch (start us, length us, event | category | flops | bytes accessed | tf_op | source)
XLA Modules:
  0.0 46.1 jit_solution(9580432202028914189)
XLA Ops:
  0.6 37.1 %gather_and_invert.1 = (f32[512,2048]{1,0:T(8,128)S(1)}, f32[512,512]{1,0:T(8,128)S(1)}, f32[512,512]{1,0:T(8,128)S(1)}, f32[2048,512]{1,0:T(8,128)S(1)}) custom-call(f32[2,512]{1,0:T(2,128)} %locs_hbm.1, f32[2,2048]{1,0:T(2,128)} %row_locs_hbm.1, f32[32,2048]{1,0:T(8,128)} %bitcast.1, f32[2048,512]{1,0:T(8,128)} %trail_ref.1), custom_call_target="tpu_custom_call" | custom-call | flops 268435456 | bytes 2097152 | tf_op jit(solution)/shard_map/gather_and_invert/pallas_call | solution.py:495
  37.8 8.1 %trailing_update.1 = (f32[2048,512]{1,0:T(8,128)}, f32[2048,512]{1,0:T(8,128)}) custom-call(f32[512,2048]{1,0:T(8,128)S(1)} %get-tuple-element.6.panel_ref, f32[512,512]{1,0:T(8,128)S(1)} %get-tuple-element.7.tile_ref, f32[512,512]{1,0:T(8,128)S(1)} %get-tuple-element.8.inv_ref, f32[2048,512]{1,0:T(8,128)S(1)} %get-tuple-element.9.gap_ref), custom_call_target="tpu_custom_call" | custom-call | flops 6442450944 | bytes 16777216 | tf_op jit(solution)/shard_map/trailing_update/pallas_call | solution.py:165

commit v5 on v4

--- a/solution.py
+++ b/solution.py
@@ -7,7 +7,7 @@
 
 STRIP = 16
 AHEAD = 2
-HAND_OVER = 2
+HAND_OVER = 1
 BLOCK = 128
 VMEM_A = 24 * 2**20
 VMEM_B = 24 * 2**20
@@ -130,15 +130,9 @@
     return jnp.concatenate([top, bottom], axis=1)
 
 
-def trailing_kernel(panel_ref, tile_ref, inv_ref, gap_ref, factor_ref, out_ref, factor_buf, out_buf, tile_buf, col_h, col_l, inv_h, inv_l, sems):
+def trailing_kernel(panel_ref, tile_ref, inv_h, inv_l, gap_ref, factor_ref, out_ref, factor_buf, out_buf, col_h, col_l, sems):
     rows = panel_ref.shape[1]
-    inv_h[...], inv_l[...] = split2(inv_ref[...])
-    col = lax.axis_index("col")
-    piece = tile_ref.shape[0] // 16
-    for r in range(16):
-        at = pl.ds(pl.multiple_of(piece_column(r, col) * piece, piece), piece)
-        tile_buf[at, :] = tile_ref[r * piece : (r + 1) * piece, :]
-    col_h[...], col_l[...] = split2(times_lower(jnp.transpose(tile_buf[...]), inv_h, inv_l))
+    col_h[...], col_l[...] = split2(times_lower(jnp.transpose(tile_ref[...]), inv_h, inv_l))
 
     def out_copy(buf, ref, which, i):
         at = pl.ds(i * ROW_TILE, ROW_TILE)
@@ -157,7 +151,7 @@
         out_copy(out_buf, out_ref, 1, i).wait()
 
 
-def trailing_update(panel_t, tile_t, inv_lower, gap):
+def trailing_update(panel_t, tile_t, inv_high, inv_low, gap):
     depth, rows = panel_t.shape
     width = gap.shape[1]
     vmem = pl.BlockSpec(memory_space=pltpu.VMEM)
@@ -165,28 +159,25 @@
     return pl.pallas_call(
         trailing_kernel,
         out_shape=(jax.ShapeDtypeStruct((rows, depth), f32), jax.ShapeDtypeStruct((rows, width), f32)),
-        in_specs=[vmem] * 4,
+        in_specs=[vmem] * 5,
         out_specs=(anywhere, anywhere),
         scratch_shapes=[
             pltpu.VMEM((rows, depth), f32),
             pltpu.VMEM((rows, width), f32),
-            pltpu.VMEM((depth, width), f32),
             pltpu.VMEM((width, depth), bf16),
             pltpu.VMEM((width, depth), bf16),
-            pltpu.VMEM((depth, depth), bf16),
-            pltpu.VMEM((depth, depth), bf16),
             pltpu.SemaphoreType.DMA((2, rows // ROW_TILE)),
         ],
         compiler_params=pltpu.CompilerParams(vmem_limit_bytes=VMEM_B),
         cost_estimate=pl.CostEstimate(flops=12 * rows * depth * width, bytes_accessed=16 * rows * width, transcendentals=0),
         name="trailing_update",
-    )(panel_t, tile_t, inv_lower, gap)
+    )(panel_t, tile_t, inv_high, inv_low, gap)
 
 
 MESH = pl.DeviceIdType.MESH
 
 
-def invert_step(k, blocks, m_ref, d_ref, inv_ref, hand_over, beside):
+def invert_step(k, blocks, m_ref, d_ref, inv_h, inv_l, hand_over, beside):
     n = m_ref.shape[1]
     lower = lax.broadcasted_iota(jnp.int32, (BLOCK, BLOCK), 0) >= lax.broadcasted_iota(jnp.int32, (BLOCK, BLOCK), 1)
     lane_block = lax.broadcasted_iota(jnp.int32, (BLOCK, n), 1) // BLOCK
@@ -197,7 +188,7 @@
     m_ref[mine, :] = hdot(w, m_ref[mine, :], ((1,), (0,)))
     m_ref[mine, mine] = w
     row = m_ref[mine, :]
-    inv_ref[mine, :] = jnp.where(lane_block <= k, row, 0.0)
+    inv_h[mine, :], inv_l[mine, :] = split2(jnp.where(lane_block <= k, row, 0.0))
 
     def below(i, carry):
         his = pl.ds(pl.multiple_of(i * BLOCK, BLOCK), BLOCK)
@@ -239,9 +230,9 @@
 
 def gather_kernel(
     locs_hbm, row_locs_hbm, prior_hbm, trail_ref,
-    panel_ref, tile_ref, inv_ref, gap_ref,
+    panel_ref, tile_ref, inv_h, inv_l, gap_ref,
     m_ref, d_ref, part_ref, turn_ref, trail_buf, col_locs_ref, locs_ref, row_locs_ref, prior_ref, trail_sems, in_sems,
-    slice_send, slice_recv, piece_send, piece_recv, pair_send, pair_recv, swap_send, locs_recv, own_sem,
+    slice_send, slice_recv, piece_send, piece_recv, swap_send, locs_recv, own_sem,
 ):
     n = locs_ref.shape[1]
     width, rows = prior_ref.shape
@@ -280,7 +271,7 @@
         trail_copy(trail_ref, trail_buf, trail_sems, b).start()
     for c in [sibling, partner] + y_own[:2]:
         pl.semaphore_signal(barrier, inc=1, device_id=(row, c), device_id_type=MESH)
-    for r in z_rows[:2] + x_rows[:2]:
+    for r in z_rows + x_rows[:2]:
         pl.semaphore_signal(barrier, inc=1, device_id=(r, col), device_id_type=MESH)
 
     @pl.when(jnp.logical_not(alone))
@@ -301,7 +292,7 @@
             part_ref[:, s] = value - prior_ref[:, s]
 
     fill_part(0, tile)
-    pl.semaphore_wait(barrier, jnp.where(alone, 8, 9))
+    pl.semaphore_wait(barrier, jnp.where(alone, 9, 10))
 
     def cut(ref, index, size, half):
         if half is None:
@@ -312,7 +303,7 @@
         return cut(panel_ref, c, width, half)
 
     def piece_of(r, half=None):
-        return cut(tile_ref, r, width, half)
+        return cut(tile_ref, piece_column(r, col), width, half)
 
     sent = []
 
@@ -344,7 +335,7 @@
     own_copy = pltpu.make_async_copy(part_ref, slice_of(col), own_sem)
     swap_src = part_ref.at[:, 0:tile]
     locs_src = row_locs_ref.at[:, 0:tile]
-    swap_copy = pltpu.make_async_remote_copy(src_ref=swap_src, dst_ref=piece_of(swap_to[0]), send_sem=swap_send.at[0], recv_sem=piece_recv.at[swap_to[0], 0], device_id=swap_to, device_id_type=MESH)
+    swap_copy = pltpu.make_async_remote_copy(src_ref=swap_src, dst_ref=cut(tile_ref, col, width, None), send_sem=swap_send.at[0], recv_sem=piece_recv.at[swap_to[0], 0], device_id=swap_to, device_id_type=MESH)
     locs_copy = pltpu.make_async_remote_copy(src_ref=locs_src, dst_ref=col_locs_ref, send_sem=swap_send.at[1], recv_sem=locs_recv, device_id=swap_to, device_id_type=MESH)
 
     @pl.when(jnp.logical_not(alone))
@@ -368,7 +359,7 @@
 
     def tile_on():
         arrived(piece_of, piece_recv, row)
-        for r in z_rows[:2] + x_rows[:2]:
+        for r in z_rows[:3] + x_rows[:2]:
             send_piece(row, r)
 
     def partner_to_y():
@@ -388,46 +379,52 @@
             arrived(slice_of, slice_recv, sources[h], 1 - h)
             send_slice(sources[h], sibling)
 
-    def opposite_slice(c):
-        for h in (0, 1):
-            arrived(slice_of, slice_recv, c, h)
-        send_slice(c, sibling)
+    def opposite_own():
+        for h in (0, 1):
+            arrived(slice_of, slice_recv, y_own[2], h)
+        send_slice(y_own[2], partner)
+        send_slice(y_own[2], sibling)
+
+    def far_over():
+        for h in (0, 1):
+            for part in (h, 1 - h):
+                arrived(slice_of, slice_recv, y_far[h], part)
+            send_slice(y_far[h], sibling)
+
+    def opposite_far():
+        arrived(slice_of, slice_recv, y_far[2])
+        send_slice(y_far[2], sibling)
+
+    def across_x(zs):
+        for z in zs:
+            for h in (0, 1):
+                arrived(piece_of, piece_recv, x_near[h] * 4 + z)
+                send_piece(x_near[h] * 4 + z, x_rows[1 - h], half=h)
 
     def pieces_on():
         for h in (0, 1):
             arrived(piece_of, piece_recv, z_rows[h])
-            send_piece(z_rows[h], z_rows[1 - h], half=h)
             for r in x_rows[:2]:
                 send_piece(z_rows[h], r)
 
     def opposite_piece():
-        for h in (0, 1):
-            arrived(piece_of, piece_recv, z_rows[2], h)
+        arrived(piece_of, piece_recv, z_rows[2])
         for r in x_rows[:2]:
             send_piece(z_rows[2], r)
-
-    def pair_of(b, half):
-        return cut(tile_ref, b, 4 * width, half)
-
-    def tiles_on():
-        for h in (0, 1):
-            for e in range(4):
-                arrived(piece_of, piece_recv, x_near[h] * 4 + e)
-            send(pair_of, pair_send, pair_recv, x_near[h], h, (x_rows[1 - h], col))
-
-    schedule = [(3, "own"), (4, "tile_on"), (5, "partner_to_y"), (6, "own_over"), (8, "pieces_on"), (8, "opposite_own"), (10, "far"), (11, "opposite_piece"), (12, "far_over"), (13, "tiles_on"), (15, "opposite_far")]
+        across_x([z_hi])
+
+    schedule = [(6, "own"), (7, "tile_on"), (10, "partner_to_y"), (10, "own_over"), (13, "pieces_on"), (14, "opposite_own"), (16, "opposite_piece"), (20, "far_over"), (20, "tiles_on"), (24, "opposite_far")]
     tasks = dict(
         tile_on=tile_on,
         partner_to_y=partner_to_y,
         own=lambda: pass_on(y_own),
         own_over=lambda: to_sibling(y_own),
-        far=lambda: pass_on(y_far),
-        far_over=lambda: to_sibling(y_far),
-        opposite_own=lambda: opposite_slice(y_own[2]),
-        opposite_far=lambda: opposite_slice(y_far[2]),
+        far_over=far_over,
+        opposite_own=opposite_own,
+        opposite_far=opposite_far,
         pieces_on=pieces_on,
         opposite_piece=opposite_piece,
-        tiles_on=tiles_on,
+        tiles_on=lambda: across_x(near(z_hi)),
     )
     stages = {}
     for stage, name in schedule:
@@ -454,13 +451,13 @@
         if place + 1 < blocks:
             fill_matrix(locs_ref, m_ref, n, place + 1)
 
-    invert_step(0, blocks, m_ref, d_ref, inv_ref, hand_over(0, 1), fill_beside)
+    invert_step(0, blocks, m_ref, d_ref, inv_h, inv_l, hand_over(0, 1), fill_beside)
     wait_bytes(col_locs_ref, locs_recv)
     for part in range(TRAIL_PARTS):
         trail_copy(trail_ref, trail_buf, trail_sems, part).wait()
 
     def one_block(k, carry):
-        invert_step(k, blocks, m_ref, d_ref, inv_ref, hand_over(1, blocks), beside)
+        invert_step(k, blocks, m_ref, d_ref, inv_h, inv_l, hand_over(1, blocks), beside)
         return carry
 
     lax.fori_loop(1, blocks, one_block, 0)
@@ -472,8 +469,9 @@
     for a in range(2):
         for b in range(4):
             arrived(slice_of, slice_recv, col_of(a, b, 1 - core))
-    for h in (0, 1):
-        wait_bytes(pair_of(x_near[2], h), pair_recv.at[x_near[2], h])
+    for z in range(4):
+        for h in (0, 1):
+            arrived(piece_of, piece_recv, x_near[2] * 4 + z, h)
     own_copy.wait()
     for of, sends, slot, half in sent:
         wait_bytes(of(0, half), sends.at[slot])
@@ -497,11 +495,12 @@
         out_shape=(
             jax.ShapeDtypeStruct((n, rows), f32),
             jax.ShapeDtypeStruct((n, tile), f32),
-            jax.ShapeDtypeStruct((n, n), f32),
+            jax.ShapeDtypeStruct((n, n), bf16),
+            jax.ShapeDtypeStruct((n, n), bf16),
             jax.ShapeDtypeStruct((rows, tile), f32),
         ),
         in_specs=[pl.BlockSpec(memory_space=pltpu.HBM)] * 4,
-        out_specs=(vmem, vmem, vmem, vmem),
+        out_specs=(vmem,) * 5,
         scratch_shapes=[
             pltpu.VMEM((n, n), f32),
             pltpu.VMEM((BLOCK, BLOCK), f32),
@@ -514,7 +513,7 @@
             pltpu.VMEM((width, rows), f32),
             dma((TRAIL_PARTS,)),
             dma((3,)),
-            dma((21,)), dma((n_col, 2)), dma((12,)), dma((n_col, 2)), dma((2,)), dma((4, 2)), dma((2,)), dma, dma,
+            dma((20,)), dma((n_col, 2)), dma((19,)), dma((n_col, 2)), dma((2,)), dma, dma,
         ],
         compiler_params=pltpu.CompilerParams(vmem_limit_bytes=VMEM_A, collective_id=0, has_side_effects=True),
         cost_estimate=pl.CostEstimate(flops=2 * n**3, bytes_accessed=8 * n * n, transcendentals=n * n),

time: 46.2 us -> 46.3 us (level)
  no operation moved by 1% of the time
where the time goes in v5:
time: 46.3 us; the launch traced here: 46.2 us
  Pallas kernels  45.4 us (98%)
  between operations  0.8 us (2%)
    pallas_call x1, Pallas kernels, gather_and_invert(): pl.pallas_call(gather_kernel, out_shape=(jax.ShapeDtypeStruct((n, rows),...  37.4 us
    pallas_call x1, Pallas kernels, trailing_update(): pl.pallas_call(trailing_kernel, out_shape=(jax.ShapeDtypeStruct((rows, de...  8 us

profile of v5, /device:TPU:1, one launch (start us, length us, event | category | flops | bytes accessed | tf_op | source)
XLA Modules:
  0.0 46.2 jit_solution(10460719471919408544)
XLA Ops:
  0.6 37.4 %gather_and_invert.1 = (f32[512,2048]{1,0:T(8,128)S(1)}, f32[512,512]{1,0:T(8,128)S(1)}, bf16[512,512]{1,0:T(8,128)(2,1)S(1)}, bf16[512,512]{1,0:T(8,128)(2,1)S(1)}, f32[2048,512]{1,0:T(8,128)S(1)}) custom-call(f32[2,512]{1,0:T(2,128)} %locs_hbm.1, f32[2,2048]{1,0:T(2,128)} %row_locs_hbm.1, f32[32,2048]{1,0:T(8,128)} %bitcast.1, f32[2048,512]{1,0:T(8,128)} %trail_ref.1), custom_call_target="tpu_custom_call" | custom-call | flops 268435456 | bytes 2097152 | tf_op jit(solution)/shard_map/gather_and_invert/pallas_call | solution.py:493
  38.1 8.0 %trailing_update.1 = (f32[2048,512]{1,0:T(8,128)}, f32[2048,512]{1,0:T(8,128)}) custom-call(f32[512,2048]{1,0:T(8,128)S(1)} %get-tuple-element.7.panel_ref, f32[512,512]{1,0:T(8,128)S(1)} %get-tuple-element.8.tile_ref, bf16[512,512]{1,0:T(8,128)(2,1)S(1)} %get-tuple-element.9.inv_h, bf16[512,512]{1,0:T(8,128)(2,1)S(1)} %get-tuple-element.10.inv_l, ...), custom_call_target="tpu_custom_call" | custom-call | flops 6442450944 | bytes 16777216 | tf_op jit(solution)/shard_map/trailing_update/pallas_call | solution.py:159

commit v6 on v4

--- a/solution.py
+++ b/solution.py
@@ -130,9 +130,8 @@
     return jnp.concatenate([top, bottom], axis=1)
 
 
-def trailing_kernel(panel_ref, tile_ref, inv_ref, gap_ref, factor_ref, out_ref, factor_buf, out_buf, tile_buf, col_h, col_l, inv_h, inv_l, sems):
+def trailing_kernel(panel_ref, tile_ref, inv_h, inv_l, gap_ref, factor_ref, out_ref, factor_buf, out_buf, tile_buf, col_h, col_l, sems):
     rows = panel_ref.shape[1]
-    inv_h[...], inv_l[...] = split2(inv_ref[...])
     col = lax.axis_index("col")
     piece = tile_ref.shape[0] // 16
     for r in range(16):
@@ -157,7 +156,7 @@
         out_copy(out_buf, out_ref, 1, i).wait()
 
 
-def trailing_update(panel_t, tile_t, inv_lower, gap):
+def trailing_update(panel_t, tile_t, inv_high, inv_low, gap):
     depth, rows = panel_t.shape
     width = gap.shape[1]
     vmem = pl.BlockSpec(memory_space=pltpu.VMEM)
@@ -165,7 +164,7 @@
     return pl.pallas_call(
         trailing_kernel,
         out_shape=(jax.ShapeDtypeStruct((rows, depth), f32), jax.ShapeDtypeStruct((rows, width), f32)),
-        in_specs=[vmem] * 4,
+        in_specs=[vmem] * 5,
         out_specs=(anywhere, anywhere),
         scratch_shapes=[
             pltpu.VMEM((rows, depth), f32),
@@ -173,20 +172,18 @@
             pltpu.VMEM((depth, width), f32),
             pltpu.VMEM((width, depth), bf16),
             pltpu.VMEM((width, depth), bf16),
-            pltpu.VMEM((depth, depth), bf16),
-            pltpu.VMEM((depth, depth), bf16),
             pltpu.SemaphoreType.DMA((2, rows // ROW_TILE)),
         ],
         compiler_params=pltpu.CompilerParams(vmem_limit_bytes=VMEM_B),
         cost_estimate=pl.CostEstimate(flops=12 * rows * depth * width, bytes_accessed=16 * rows * width, transcendentals=0),
         name="trailing_update",
-    )(panel_t, tile_t, inv_lower, gap)
+    )(panel_t, tile_t, inv_high, inv_low, gap)
 
 
 MESH = pl.DeviceIdType.MESH
 
 
-def invert_step(k, blocks, m_ref, d_ref, inv_ref, hand_over, beside):
+def invert_step(k, blocks, m_ref, d_ref, inv_h, inv_l, hand_over, beside):
     n = m_ref.shape[1]
     lower = lax.broadcasted_iota(jnp.int32, (BLOCK, BLOCK), 0) >= lax.broadcasted_iota(jnp.int32, (BLOCK, BLOCK), 1)
     lane_block = lax.broadcasted_iota(jnp.int32, (BLOCK, n), 1) // BLOCK
@@ -197,7 +194,7 @@
     m_ref[mine, :] = hdot(w, m_ref[mine, :], ((1,), (0,)))
     m_ref[mine, mine] = w
     row = m_ref[mine, :]
-    inv_ref[mine, :] = jnp.where(lane_block <= k, row, 0.0)
+    inv_h[mine, :], inv_l[mine, :] = split2(jnp.where(lane_block <= k, row, 0.0))
 
     def below(i, carry):
         his = pl.ds(pl.multiple_of(i * BLOCK, BLOCK), BLOCK)
@@ -239,7 +236,7 @@
 
 def gather_kernel(
     locs_hbm, row_locs_hbm, prior_hbm, trail_ref,
-    panel_ref, tile_ref, inv_ref, gap_ref,
+    panel_ref, tile_ref, inv_h, inv_l, gap_ref,
     m_ref, d_ref, part_ref, turn_ref, trail_buf, col_locs_ref, locs_ref, row_locs_ref, prior_ref, trail_sems, in_sems,
     slice_send, slice_recv, piece_send, piece_recv, pair_send, pair_recv, swap_send, locs_recv, own_sem,
 ):
@@ -454,13 +451,13 @@
         if place + 1 < blocks:
             fill_matrix(locs_ref, m_ref, n, place + 1)
 
-    invert_step(0, blocks, m_ref, d_ref, inv_ref, hand_over(0, 1), fill_beside)
+    invert_step(0, blocks, m_ref, d_ref, inv_h, inv_l, hand_over(0, 1), fill_beside)
     wait_bytes(col_locs_ref, locs_recv)
     for part in range(TRAIL_PARTS):
         trail_copy(trail_ref, trail_buf, trail_sems, part).wait()
 
     def one_block(k, carry):
-        invert_step(k, blocks, m_ref, d_ref, inv_ref, hand_over(1, blocks), beside)
+        invert_step(k, blocks, m_ref, d_ref, inv_h, inv_l, hand_over(1, blocks), beside)
         return carry
 
     lax.fori_loop(1, blocks, one_block, 0)
@@ -497,11 +494,12 @@
         out_shape=(
             jax.ShapeDtypeStruct((n, rows), f32),
             jax.ShapeDtypeStruct((n, tile), f32),
-            jax.ShapeDtypeStruct((n, n), f32),
+            jax.ShapeDtypeStruct((n, n), bf16),
+            jax.ShapeDtypeStruct((n, n), bf16),
             jax.ShapeDtypeStruct((rows, tile), f32),
         ),
         in_specs=[pl.BlockSpec(memory_space=pltpu.HBM)] * 4,
-        out_specs=(vmem, vmem, vmem, vmem),
+        out_specs=(vmem,) * 5,
         scratch_shapes=[
             pltpu.VMEM((n, n), f32),
             pltpu.VMEM((BLOCK, BLOCK), f32),

time: 46.2 us -> 46.2 us (level)
  no operation moved by 1% of the time
where the time goes in v6:
time: 46.2 us; the launch traced here: 46.1 us
  Pallas kernels  45.3 us (98%)
  between operations  0.8 us (2%)
    pallas_call x1, Pallas kernels, gather_and_invert(): pl.pallas_call(gather_kernel, out_shape=(jax.ShapeDtypeStruct((n, rows),...  37.1 us
    pallas_call x1, Pallas kernels, trailing_update(): pl.pallas_call(trailing_kernel, out_shape=(jax.ShapeDtypeStruct((rows, de...  8.15 us

profile of v6, /device:TPU:1, one launch (start us, length us, event | category | flops | bytes accessed | tf_op | source)
XLA Modules:
  0.0 46.1 jit_solution(6931086214230586175)
XLA Ops:
  0.6 37.1 %gather_and_invert.1 = (f32[512,2048]{1,0:T(8,128)S(1)}, f32[512,512]{1,0:T(8,128)S(1)}, bf16[512,512]{1,0:T(8,128)(2,1)S(1)}, bf16[512,512]{1,0:T(8,128)(2,1)S(1)}, f32[2048,512]{1,0:T(8,128)S(1)}) custom-call(f32[2,512]{1,0:T(2,128)} %locs_hbm.1, f32[2,2048]{1,0:T(2,128)} %row_locs_hbm.1, f32[32,2048]{1,0:T(8,128)} %bitcast.1, f32[2048,512]{1,0:T(8,128)} %trail_ref.1), custom_call_target="tpu_custom_call" | custom-call | flops 268435456 | bytes 2097152 | tf_op jit(solution)/shard_map/gather_and_invert/pallas_call | solution.py:492
  37.8 8.1 %trailing_update.1 = (f32[2048,512]{1,0:T(8,128)}, f32[2048,512]{1,0:T(8,128)}) custom-call(f32[512,2048]{1,0:T(8,128)S(1)} %get-tuple-element.7.panel_ref, f32[512,512]{1,0:T(8,128)S(1)} %get-tuple-element.8.tile_ref, bf16[512,512]{1,0:T(8,128)(2,1)S(1)} %get-tuple-element.9.inv_h, bf16[512,512]{1,0:T(8,128)(2,1)S(1)} %get-tuple-element.10.inv_l, ...), custom_call_target="tpu_custom_call" | custom-call | flops 6442450944 | bytes 16777216 | tf_op jit(solution)/shard_map/trailing_update/pallas_call | solution.py:164
